TPU v7x, 32 devices: a whole 2x2x4 slice. The times are simulated.
32 devices in a mesh: shot: 8 (over z, x), line: 4 (over y, core).
Axes of the slice: x: 2, y: 2, z: 4, core: 2. Of those that a mesh axis runs over, the one named last changes fastest.
Arguments:
- data: bfloat16 [8, 8, 256, 1024], P('shot', 'line'), may hold values from -6 to 6
- live_mask: int32 [8, 8, 256], P('shot', 'line'), may hold values 0 or 1
- patch_start: int32 [8, 8], replicated, may hold values from 0 to 256
- receiver_slot: int32 [8, 512], P('line'), may hold values from 0 to 511, each once within a row
- shot_kernels: bfloat16 [6, 3, 5, 31], replicated, may hold values from -0.25 to 0.25
- shot_tau: float32 [6], replicated, may hold values from 0.2 to 2
- receiver_kernels: bfloat16 [6, 5, 31], replicated, may hold values from -0.5 to 0.5
- receiver_tau: float32 [6], replicated, may hold values from 0.2 to 2
Outputs:
- receiver_gathers: bfloat16 [8, 512, 8, 1024], P('line', 'shot')
Inputs may be any that keep to these rules, and one draw needn't show every extreme that they name: Each row of receiver_slot names every slot once.
All inputs are finite; a program needn't handle non-finite values. No bound on the sum of `live_mask` on one device may be relied on, other than what follows from the above.
Results may differ from a plain program's by a relative error of at most 0.0051.
Values may be sent and summed in bfloat16 or wider, within the bound.
A program may use at most 192 MiB of HBM per device.

v0:
```python
import jax
import jax.numpy as jnp
from jax import lax
from jax.sharding import PartitionSpec as P


def extended(cells, sides, width):
    for axis, dim in sides:
        count = lax.axis_size(axis)
        ends = count - 1
        head = lax.slice_in_dim(cells, 0, width, axis=dim)
        tail = lax.slice_in_dim(cells, cells.shape[dim] - width, cells.shape[dim], axis=dim)
        cells = jnp.concatenate(
            [
                lax.ppermute(tail, axis, [(i, (i + 1) % count) for i in range(ends)]),
                cells,
                lax.ppermute(head, axis, [((i + 1) % count, i) for i in range(ends)]),
            ],
            axis=dim,
        )
    return cells


def time_windows(slab):
    stride = 97
    samples = slab.shape[-1]
    num_blocks = (samples + stride - 1) // stride
    total = num_blocks * stride
    lead = slab.shape[:-1]
    padded = jnp.pad(slab, [(0, 0)] * (slab.ndim - 1) + [(15, total - samples + stride - 15)])
    head_part = padded[..., :total].reshape(lead + (num_blocks, stride))
    tail_part = padded[..., stride : stride + total].reshape(lead + (num_blocks, stride))[
        ..., : 128 - stride
    ]
    return jnp.concatenate([head_part, tail_part], axis=-1)


def unwindow(blocks, samples):
    stride = 97
    lead = blocks.shape[:-2]
    return blocks[..., :stride].reshape(lead + (blocks.shape[-2] * stride,))[..., :samples]


def tap_matrix(kernels):
    stride = 97
    lanes = 128
    bank = kernels.shape[0]
    taps = kernels.shape[-1]
    flat = kernels.reshape(bank, -1, taps)
    window_pos = jnp.arange(lanes, dtype=jnp.int32)[:, None, None]
    out_pos = jnp.arange(lanes, dtype=jnp.int32)[None, :, None]
    tap_ids = jnp.arange(taps, dtype=jnp.int32)[None, None, :]
    onehot = ((window_pos - out_pos == tap_ids) & (out_pos < stride)).astype(jnp.bfloat16)
    matrix = jnp.einsum("kot,wut->owku", flat, onehot, preferred_element_type=jnp.float32)
    return matrix.reshape(flat.shape[1] * lanes, bank * lanes).astype(jnp.bfloat16)


def shrink_sum(filtered, tau):
    tau_sq = (tau * tau)[:, None]
    return jnp.sum(filtered * filtered * filtered / (filtered * filtered + tau_sq), axis=-2)


def per_device(
    data,
    live_mask,
    patch_start,
    receiver_slot,
    shot_kernels,
    shot_tau,
    receiver_kernels,
    receiver_tau,
):
    shot_dev, lines_dev, channels, samples = data.shape
    stations = receiver_slot.shape[1]
    shot_count = patch_start.shape[0]
    first_shot = lax.axis_index("shot") * shot_dev
    first_line = lax.axis_index("line") * lines_dev
    bank_one = shot_kernels.shape[0]
    bank_two = receiver_kernels.shape[0]
    shot_matrix = tap_matrix(shot_kernels)
    recv_matrix = tap_matrix(receiver_kernels)
    live_data = data * live_mask[..., None].astype(jnp.bfloat16)
    with_rims = extended(live_data, (("line", 1),), 1)
    station_ids = jnp.arange(stations, dtype=jnp.int32)
    line_rows = jnp.arange(lines_dev, dtype=jnp.int32)[:, None]
    slot_station = (
        jnp.zeros((lines_dev, stations), jnp.int32)
        .at[line_rows, receiver_slot]
        .set(jnp.broadcast_to(station_ids[None, :], (lines_dev, stations)))
    )
    start_cols = lax.dynamic_slice_in_dim(patch_start, first_line, lines_dev, 1)
    chan_all = station_ids[None, None, :] - start_cols[:, :, None]
    covered_all = (chan_all >= 0) & (chan_all < channels)
    fold_all = jnp.cumsum(covered_all.astype(jnp.int32), axis=0) - 1
    fold_all = jnp.where(covered_all, fold_all, -1)
    fold_own = lax.dynamic_slice_in_dim(fold_all, first_shot, shot_dev, 0)
    chan_own = lax.dynamic_slice_in_dim(chan_all, first_shot, shot_dev, 0)
    fold_slot = jnp.take_along_axis(fold_own, slot_station[None], axis=2)
    chan_slot = jnp.take_along_axis(chan_own, slot_station[None], axis=2)
    padded = jnp.pad(with_rims[0, 0 : 0 + lines_dev + 2], ((0, 0), (2, 2), (0, 0)))
    windows = time_windows(padded)
    slab_list = []
    for line_off in range(3):
        for chan_off in range(5):
            slab_list.append(
                windows[line_off : line_off + lines_dev, chan_off : chan_off + channels]
            )
    stacked = jnp.stack(slab_list, axis=-2)
    lead = stacked.shape[:3]
    filtered = jnp.dot(
        stacked.reshape(-1, 15 * 128), shot_matrix, preferred_element_type=jnp.float32
    )
    filtered = filtered.reshape(lead + (bank_one, 128))
    noise_est = unwindow(shrink_sum(filtered, shot_tau), samples)
    weight_mask = live_mask[0, 0 : 0 + lines_dev].astype(jnp.float32)[..., None]
    results = [
        ((live_data[0, 0 : 0 + lines_dev].astype(jnp.float32) - noise_est) * weight_mask).astype(
            jnp.bfloat16
        )
    ]
    cleaned = jnp.stack(results)
    inside = (chan_slot >= 0) & (chan_slot < channels)
    clipped = jnp.clip(chan_slot, 0, channels - 1)
    picked = jnp.take_along_axis(cleaned, clipped[..., None], axis=2)
    picked = picked * inside[..., None].astype(jnp.bfloat16)
    regroup_traces = lax.all_to_all(picked, "shot", split_axis=2, concat_axis=0, tiled=True)
    regroup_fold_ids = lax.all_to_all(fold_slot, "shot", split_axis=2, concat_axis=0, tiled=True)
    fold_range = jnp.arange(shot_count, dtype=jnp.int32)
    onehot = (regroup_fold_ids[..., None] == fold_range).astype(jnp.bfloat16)
    gathered = jnp.einsum(
        "snrf,snrt->nrft", onehot, regroup_traces, preferred_element_type=jnp.float32
    ).astype(jnp.bfloat16)
    live_count = jnp.sum((regroup_fold_ids >= 0).astype(jnp.int32), axis=0)
    live_fold = (fold_range[None, None, :] < live_count[..., None]).astype(jnp.float32)
    padded = jnp.pad(gathered, ((0, 0), (0, 0), (2, 2), (0, 0)))
    windows = time_windows(padded)
    slab_list = [windows[:, :, fold_off : fold_off + shot_count] for fold_off in range(5)]
    stacked = jnp.stack(slab_list, axis=-2)
    lead = stacked.shape[:4]
    filtered = jnp.dot(
        stacked.reshape(-1, 5 * 128), recv_matrix, preferred_element_type=jnp.float32
    )
    filtered = filtered.reshape(lead + (bank_two, 128))
    noise_est = unwindow(shrink_sum(filtered, receiver_tau), samples)
    return ((gathered.astype(jnp.float32) - noise_est) * live_fold[..., None]).astype(jnp.bfloat16)


def solution(mesh):
    return jax.shard_map(
        per_device,
        mesh=mesh,
        in_specs=(
            P("shot", "line", None, None),
            P("shot", "line", None),
            P(),
            P("line", None),
            P(),
            P(),
            P(),
            P(),
        ),
        out_specs=P("line", "shot", None, None),
        check_vma=False,
    )
```

profile of v0, /device:TPU:0, one launch (start us, length us, event | category | flops | bytes accessed | tf_op | source)
XLA Modules:
  0.0 381.4 jit_solution(13325841418651990846)
XLA Ops:
  4.2 3.2 collective-permute-start
  10.0 4.3 %scatter_custom_fusion = s32[1024]{0:T(1024)S(1)} fusion(s32[1024]{0:T(1024)S(1)} %bitcast.258, s32[1024]{0:T(1024)S(1)} %bitcast.259, s32[]{:T(128)} %constant.22.clone.1), kind=kCustom, calls=%fused_computation.127 | custom fusion | bytes 4100
  14.3 9.1 %gather_fusion.1 = s32[1024]{0:T(1024)S(1)} fusion(s32[2,512]{1,0:T(2,128)S(1)} %get-tuple-element.16, s32[1024]{0:T(1024)S(1)} %bitcast.233), kind=kCustom, calls=%fused_computation.clone | custom fusion | bytes 16384 | tf_op jit(solution)/shard_map/jit(take_along_axis)/gather | solution.py:98
  26.3 7.2 %all-to-all-start = ((s32[8,1,128]{2,1,0:T(1,128)}), s32[8,1,128]{2,1,0:T(1,128)S(1)}, u32[]{:S(2)}, u32[]{:S(2)}) async-start(s32[8,1,128]{2,1,0:T(1,128)} %reshape.270), calls=%async_computation | async-start | bytes 8192 | tf_op jit(solution)/shard_map/all_to_all | solution.py:127
  33.5 9.1 %gather_fusion.2 = s32[1024]{0:T(1024)S(1)} fusion(s32[2,512]{1,0:T(2,128)S(1)} %get-tuple-element.17, s32[1024]{0:T(1024)S(1)} %bitcast.234), kind=kCustom, calls=%fused_computation.1.clone | custom fusion | bytes 16384 | tf_op jit(solution)/shard_map/jit(take_along_axis)/gather | solution.py:99
  43.7 4.0 %copy.111 = bf16[15,128,6,128]{1,0,3,2:T(8,128)(2,1)} copy(bf16[15,128,6,128]{3,0,2,1:T(8,128)(2,1)S(1)} %convert_bitcast_fusion) | data formatting | bytes 5898240 | tf_op jit(solution)/shard_map/convert_element_type | solution.py:55
  47.7 4.8 %copy.162 = bf16[96,8,15,128]{3,1,2,0:T(8,128)(2,1)} copy(bf16[96,8,15,128]{3,2,1,0:T(8,128)(2,1)} %bitcast.244) | data formatting | bytes 5898240
  55.6 5.3 %pad_slice_fusion.2 = (bf16[4,260,1067]{2,1,0:T(8,128)(2,1)S(1)}, bf16[4,260,1067]{2,1,0:T(8,128)(2,1)}) fusion(bf16[4,256,1024]{2,1,0:T(8,128)(2,1)S(1)} %maximum_bitcast_fusion.18), kind=kLoop, calls=%fused_computation.34 | loop fusion | bytes 6535872 | tf_op jit(solution)/shard_map/slice | solution.py:31
  60.8 8.1 %reshape.191 = bf16[4,260,11,97]{3,2,1,0:T(8,128)(2,1)} reshape(bf16[4,260,1067]{2,1,0:T(8,128)(2,1)} %get-tuple-element.11) | data formatting | bytes 4438720 | tf_op jit(solution)/shard_map/reshape | solution.py:32
  68.9 7.3 %reshape.190 = bf16[4,260,11,97]{3,2,1,0:T(8,128)(2,1)} reshape(bf16[4,260,1067]{2,1,0:T(8,128)(2,1)S(1)} %get-tuple-element.10) | data formatting | bytes 4438720 | tf_op jit(solution)/shard_map/reshape | solution.py:31
  76.2 5.0 %fusion.31 = bf16[2,256,11,15,128]{4,2,1,0,3:T(8,128)(2,1)} fusion(bf16[4,260,11,31]{3,2,1,0:T(8,128)(2,1)} %bitcast.216, bf16[4,260,11,97]{3,2,1,0:T(8,128)(2,1)} %reshape.190), kind=kLoop, calls=%fused_computation.67 | loop fusion | flops 2883583 | bytes 5025792
  81.2 2.6 fusion.30
  83.8 2.6 fusion.29
  86.4 2.6 fusion.28
  89.1 2.7 fusion.27
  91.7 2.6 fusion.26
  94.3 2.6 fusion.25
  96.9 2.6 fusion.24
  99.5 2.8 fusion.23
  102.3 2.6 fusion.22
  104.9 2.6 fusion.21
  107.5 2.6 fusion.20
  110.1 2.7 fusion.19
  112.8 2.6 fusion.18
  115.4 2.6 fusion.17
  118.0 37.5 %copy.108 = bf16[2,256,11,15,128]{1,4,3,2,0:T(8,128)(2,1)} copy(bf16[2,256,11,15,128]{4,2,1,0,3:T(8,128)(2,1)} %fusion.17) | data formatting | bytes 43253760 | tf_op jit(solution)/shard_map/stack | solution.py:108
  155.5 27.1 %fusion.3 = f32[2,256,11,128]{3,1,2,0:T(8,128)} fusion(f32[6]{0:T(128)S(1)} %mul.68, bf16[2,256,11,1920,1]{1,3,4,2,0:T(8,128)(2,1)} %bitcast.243, bf16[6,128,1920,1,1]{2,1,0,4,3:T(8,128)(2,1)} %bitcast.251), kind=kOutput, calls=%fused_computation.11 | convolution fusion | flops 16630349824 | bytes 27459608 | tf_op jit(solution)/shard_map/dot_general | solution.py:110
  182.6 4.5 %copy.113 = f32[2,256,11,97]{1,0,3,2:T(2,128)S(1)} copy(f32[2,256,11,97]{3,1,2,0:T(8,128)} %bitcast.252) | data formatting | bytes 4370432 | tf_op jit(solution)/shard_map/slice | solution.py:41
  189.2 2.8 copy.136
  193.6 10.0 %gather_fusion = bf16[1024,1024]{1,0:T(8,128)(2,1)S(1)} fusion(bf16[2,256,1024]{2,1,0:T(8,128)(2,1)S(1)} %fusion.35, s32[1024]{0:T(1024)S(1)} %bitcast.242), kind=kCustom, calls=%fused_computation.2 | custom fusion | bytes 4202496 | tf_op jit(solution)/shard_map/jit(take_along_axis)/gather | solution.py:124
  203.6 4.7 %fusion.15 = bf16[1,2,512,1024]{3,1,0,2:T(2,128)(2,1)} fusion(pred[2,512]{0,1:T(8,128)(4,1)S(1)} %copy-done.11, bf16[1,2,512,1024]{3,2,1,0:T(8,128)(2,1)S(1)} %bitcast.246, bf16[2,512]{0,1:T(8,128)(2,1)S(1)} %copy-done.10), kind=kLoop, calls=%fused_computation.36 | loop fusion | flops 2097152 | bytes 4197376 | tf_op jit(solution)/shard_map/mul | solution.py:125
  208.3 6.2 %all-to-all-start.1 = ((bf16[1,2,512,1024]{3,1,0,2:T(2,128)(2,1)}), bf16[1,2,512,1024]{3,1,0,2:T(2,128)(2,1)S(1)}, u32[]{:S(2)}, u32[]{:S(2)}) async-start(bf16[1,2,512,1024]{3,1,0,2:T(2,128)(2,1)} %fusion.15), calls=%async_computation.1 | async-start | bytes 4194304 | tf_op jit(solution)/shard_map/all_to_all | solution.py:126
  218.8 45.4 %all-to-all-done.1 = bf16[1,2,512,1024]{3,1,0,2:T(2,128)(2,1)S(1)} async-done(((bf16[1,2,512,1024]{3,1,0,2:T(2,128)(2,1)}), bf16[1,2,512,1024]{3,1,0,2:T(2,128)(2,1)S(1)}, u32[]{:S(2)}, u32[]{:S(2)}) %all-to-all-start.1) | async-done | bytes 2097184 | tf_op jit(solution)/shard_map/all_to_all | solution.py:126
  265.5 4.0 %fusion.39 = bf16[2,64,8,1024]{3,2,1,0:T(8,128)(2,1)S(1)} fusion(bf16[1,2,8,64,1024]{4,1,3,2,0:T(2,128)(2,1)} %bitcast.247, s32[8,2,64]{0,2,1:T(8,128)S(1)} %copy.104), kind=kOutput, calls=%fused_computation.78 | convolution fusion | flops 17833984 | bytes 4198400 | tf_op jit(solution)/shard_map/snrf,snrt->nrft/dot_general | solution.py:130
  269.5 9.3 %pad_slice_fusion = (bf16[2,64,12,1067]{3,2,1,0:T(8,128)(2,1)}, bf16[2,64,12,1067]{3,2,1,0:T(8,128)(2,1)S(1)}) fusion(bf16[2,64,8,1024]{3,2,1,0:T(8,128)(2,1)S(1)} %fusion.39), kind=kLoop, calls=%fused_computation.15 | loop fusion | bytes 8652800 | tf_op jit(solution)/shard_map/slice | solution.py:31
  278.9 2.6 copy.120
  281.4 12.2 %reshape.195 = bf16[2,64,12,11,97]{4,3,1,2,0:T(8,128)(2,1)} reshape(bf16[2,64,12,1067]{3,1,2,0:T(8,128)(2,1)} %copy.120) | data formatting | bytes 6555648 | tf_op jit(solution)/shard_map/reshape | solution.py:32
  293.6 4.9 %copy.119 = bf16[2,64,12,1067]{3,1,2,0:T(8,128)(2,1)} copy(bf16[2,64,12,1067]{3,2,1,0:T(8,128)(2,1)} %get-tuple-element.8) | data formatting | bytes 6555648 | tf_op jit(solution)/shard_map/slice | solution.py:31
  298.5 12.2 %reshape.194 = bf16[2,64,12,11,97]{4,3,1,2,0:T(8,128)(2,1)} reshape(bf16[2,64,12,1067]{3,1,2,0:T(8,128)(2,1)} %copy.119) | data formatting | bytes 6555648 | tf_op jit(solution)/shard_map/reshape | solution.py:31
  310.7 6.5 %fusion.14 = bf16[2,64,8,11,5,128]{5,3,1,2,0,4:T(8,128)(2,1)} fusion(bf16[2,64,12,11,31]{4,3,1,2,0:T(8,128)(2,1)} %bitcast.235, bf16[2,64,12,11,97]{4,3,1,2,0:T(8,128)(2,1)} %reshape.194), kind=kLoop, calls=%fused_computation.30 | loop fusion | flops 5767167 | bytes 8519680
  319.4 3.9 %fusion.13 = bf16[2,64,8,11,5,128]{5,3,1,2,0,4:T(8,128)(2,1)} fusion(bf16[2,64,8,11,5,128]{5,3,1,2,0,4:T(8,128)(2,1)} %fusion.14, bf16[2,64,12,11,31]{4,3,1,2,0:T(8,128)(2,1)S(1)} %bitcast.238, bf16[2,64,12,11,97]{4,3,1,2,0:T(8,128)(2,1)S(1)} %copy-done.3), kind=kLoop, calls=%fused_computation.28 | loop fusion | flops 5767168 | bytes 8519680
  323.3 3.9 %fusion.12 = bf16[2,64,8,11,5,128]{5,3,1,2,0,4:T(8,128)(2,1)} fusion(bf16[2,64,8,11,5,128]{5,3,1,2,0,4:T(8,128)(2,1)} %fusion.13, bf16[2,64,12,11,31]{4,3,1,2,0:T(8,128)(2,1)S(1)} %bitcast.239, bf16[2,64,12,11,97]{4,3,1,2,0:T(8,128)(2,1)S(1)} %copy-done.3), kind=kLoop, calls=%fused_computation.26 | loop fusion | flops 5767168 | bytes 8519680
  327.2 3.9 %fusion.11 = bf16[2,64,8,11,5,128]{5,3,1,2,0,4:T(8,128)(2,1)} fusion(bf16[2,64,8,11,5,128]{5,3,1,2,0,4:T(8,128)(2,1)} %fusion.12, bf16[2,64,12,11,31]{4,3,1,2,0:T(8,128)(2,1)S(1)} %bitcast.240, bf16[2,64,12,11,97]{4,3,1,2,0:T(8,128)(2,1)S(1)} %copy-done.3), kind=kLoop, calls=%fused_computation.24 | loop fusion | flops 5767168 | bytes 8519680
  331.1 3.9 %fusion.10 = bf16[2,64,8,11,5,128]{5,3,1,2,0,4:T(8,128)(2,1)} fusion(bf16[2,64,8,11,5,128]{5,3,1,2,0,4:T(8,128)(2,1)} %fusion.11, bf16[2,64,12,11,31]{4,3,1,2,0:T(8,128)(2,1)S(1)} %bitcast.241, bf16[2,64,12,11,97]{4,3,1,2,0:T(8,128)(2,1)S(1)} %copy-done.3), kind=kLoop, calls=%fused_computation.22 | loop fusion | flops 5767168 | bytes 8519680 | tf_op jit(solution)/shard_map/stack | solution.py:138
  335.0 28.7 %fusion.1 = f32[2,64,8,11,128]{4,2,3,1,0:T(8,128)S(1)} fusion(f32[6]{0:T(128)S(1)} %mul.75, bf16[6,128,640,1,1,1]{2,1,0,5,4,3:T(8,128)(2,1)S(1)} %bitcast.256, bf16[2,64,8,11,5,128]{5,3,1,2,0,4:T(8,128)(2,1)} %fusion.10), kind=kOutput, calls=%fused_computation.7 | convolution fusion | flops 11114774528 | bytes 21168152 | tf_op jit(solution)/shard_map/dot_general | solution.py:140
  363.7 4.9 %copy.124 = f32[2,64,8,11,97]{4,3,2,1,0:T(8,128)} copy(f32[2,64,8,11,97]{4,2,3,1,0:T(8,128)S(1)} %bitcast.248) | data formatting | bytes 8740864 | tf_op jit(solution)/shard_map/slice | solution.py:41
  368.6 8.4 %reshape.196 = f32[2,64,8,1067]{3,2,1,0:T(8,128)} reshape(f32[2,64,8,11,97]{4,3,2,1,0:T(8,128)} %copy.124) | data formatting | bytes 8740864 | tf_op jit(solution)/shard_map/reshape | solution.py:41
  377.0 4.1 %fusion.8 = bf16[2,64,8,1024]{3,2,1,0:T(8,128)(2,1)} fusion(f32[2,64,8,1067]{3,2,1,0:T(8,128)} %reshape.196, bf16[2,64,8,1024]{3,2,1,0:T(8,128)(2,1)S(1)} %fusion.39, f32[2,64,8]{2,1,0:T(8,128)S(1)} %fusion.58), kind=kLoop, calls=%fused_computation.19 | loop fusion | flops 4194304 | bytes 8392704 | tf_op jit(solution)/shard_map/convert_element_type | solution.py:145
  (101 shorter events, 24.9 us)
Async XLA Ops:
  0.0 214.5 %copy-start = (bf16[6,5,31]{2,0,1:T(8,128)(2,1)S(1)}, bf16[6,5,31]{2,0,1:T(8,128)(2,1)}, u32[]{:S(2)}) copy-start(bf16[6,5,31]{2,0,1:T(8,128)(2,1)} %param.16) | copy-start | bytes 5584
  0.0 9.7 %copy-start.14 = (s32[2]{0:T(128)S(1)}, s32[2]{0:T(128)}, u32[]{:S(2)}) copy-start(s32[2]{0:T(128)} %constant.76) | copy-start | bytes 28
  0.0 9.8 %copy-start.15 = (s32[2]{0:T(128)S(1)}, s32[2]{0:T(128)}, u32[]{:S(2)}) copy-start(s32[2]{0:T(128)} %constant.79) | copy-start | bytes 28
  0.0 9.7 %copy-start.13 = (s32[2,512]{1,0:T(2,128)S(1)}, s32[2,512]{1,0:T(2,128)}, u32[]{:S(2)}) copy-start(s32[2,512]{1,0:T(2,128)} %param.13) | copy-start | bytes 12292
  2.1 1.0 copy-start.4
  3.1 30.4 %copy-start.12 = (bf16[6,3,5,31]{3,1,2,0:T(4,128)(2,1)S(1)}, bf16[6,3,5,31]{3,1,2,0:T(4,128)(2,1)}, u32[]{:S(2)}) copy-start(bf16[6,3,5,31]{3,1,2,0:T(4,128)(2,1)} %param.14) | copy-start | bytes 16744
  4.2 49.9 %collective-permute-start = (bf16[1,1,256,1024]{3,2,1,0:T(8,128)(2,1)}, bf16[1,1,256,1024]{3,2,1,0:T(8,128)(2,1)}, u32[]{:S(2)}, u32[]{:S(2)}) collective-permute-start(bf16[1,1,256,1024]{3,2,1,0:T(8,128)(2,1)} %get-tuple-element.12), channel_id=1, source_target_pairs={{0,1},{1,2},{2,3},{4,5},{5,6},{6,7},{8,9},{9,10},{10,11},{12,13},{... | collective-permute-start | bytes 1572872 | tf_op jit(solution)/shard_map/ppermute | solution.py:15
  7.3 46.8 %collective-permute-start.1 = (bf16[1,1,256,1024]{3,2,1,0:T(8,128)(2,1)}, bf16[1,1,256,1024]{3,2,1,0:T(8,128)(2,1)}, u32[]{:S(2)}, u32[]{:S(2)}) collective-permute-start(bf16[1,1,256,1024]{3,2,1,0:T(8,128)(2,1)} %get-tuple-element.13), channel_id=1, source_target_pairs={{1,0},{2,1},{3,2},{5,4},{6,5},{7,6},{9,8},{10,9},{11,10},{13,12},{... | collective-permute-start | bytes 1572872 | tf_op jit(solution)/shard_map/ppermute | solution.py:17
  26.3 182.1 %all-to-all-start = ((s32[8,1,128]{2,1,0:T(1,128)}), s32[8,1,128]{2,1,0:T(1,128)S(1)}, u32[]{:S(2)}, u32[]{:S(2)}) async-start(s32[8,1,128]{2,1,0:T(1,128)} %reshape.270), calls=%async_computation | async-start | bytes 8192 | tf_op jit(solution)/shard_map/all_to_all | solution.py:127
  33.5 14.2 %copy-start.8 = (s32[128,128]{1,0:T(8,128)}, s32[128,128]{1,0:T(8,128)S(1)}, u32[]{:S(2)}) copy-start(s32[128,128]{1,0:T(8,128)S(1)} %iota_subtract_fusion) | copy-start | bytes 196612
  47.7 4.8 %copy-start.16 = (f32[6]{0:T(128)S(1)}, f32[6]{0:T(128)}, u32[]{:S(2)}) copy-start(f32[6]{0:T(128)} %param.15) | copy-start | bytes 76
  47.7 6.4 %copy-start.5 = (bf16[1,2,256,1024]{3,2,1,0:T(8,128)(2,1)S(1)}, bf16[1,2,256,1024]{3,2,1,0:T(8,128)(2,1)}, u32[]{:S(2)}) copy-start(bf16[1,2,256,1024]{3,2,1,0:T(8,128)(2,1)} %copy-done.4) | copy-start | bytes 3145732
  68.9 12.3 %slice-start = ((s8[4259840]{0:T(1024)(128)(4,1)}), s8[65536]{0:T(1024)(128)(4,1)S(1)}, s32[]{:S(2)}) async-start(s8[4259840]{0:T(1024)(128)(4,1)} %bitcast.217), calls=%async_computation.2 | async-start | bytes 131072
  76.2 5.0 %slice-start.1 = ((s8[4259840]{0:T(1024)(128)(4,1)}), s8[4194304]{0:T(1024)(128)(4,1)S(1)}, s32[]{:S(2)}) async-start(s8[4259840]{0:T(1024)(128)(4,1)} %bitcast.217), calls=%async_computation.3 | async-start | bytes 8388608
  76.2 5.0 %copy-start.2 = (bf16[4,260,11,97]{3,2,1,0:T(8,128)(2,1)S(1)}, bf16[4,260,11,97]{3,2,1,0:T(8,128)(2,1)}, u32[]{:S(2)}) copy-start(bf16[4,260,11,97]{3,2,1,0:T(8,128)(2,1)} %reshape.190) | copy-start | bytes 6658084
  193.5 10.0 %copy-start.10 = (bf16[2,512]{0,1:T(8,128)(2,1)S(1)}, bf16[2,512]{0,1:T(8,128)(2,1)}, u32[]{:S(2)}) copy-start(bf16[2,512]{0,1:T(8,128)(2,1)} %copy.116) | copy-start | bytes 6148
  193.6 10.0 %copy-start.11 = (pred[2,512]{0,1:T(8,128)(4,1)S(1)}, pred[2,512]{0,1:T(8,128)(4,1)}, u32[]{:S(2)}) copy-start(pred[2,512]{0,1:T(8,128)(4,1)} %copy.105) | copy-start | bytes 3076
  203.6 11.0 %copy-start.9 = (s32[128,128]{1,0:T(8,128)S(1)}, s32[128,128]{1,0:T(8,128)}, u32[]{:S(2)}) copy-start(s32[128,128]{1,0:T(8,128)} %copy-done.8) | copy-start | bytes 196612
  208.3 55.8 %all-to-all-start.1 = ((bf16[1,2,512,1024]{3,1,0,2:T(2,128)(2,1)}), bf16[1,2,512,1024]{3,1,0,2:T(2,128)(2,1)S(1)}, u32[]{:S(2)}, u32[]{:S(2)}) async-start(bf16[1,2,512,1024]{3,1,0,2:T(2,128)(2,1)} %fusion.15), calls=%async_computation.1 | async-start | bytes 4194304 | tf_op jit(solution)/shard_map/all_to_all | solution.py:126
  214.6 2.5 copy-start.17
  264.2 1.3 copy-start.6
  310.7 6.5 %slice-start.2 = ((s8[6291456]{0:T(1024)(128)(4,1)}), s8[4194304]{0:T(1024)(128)(4,1)S(1)}, s32[]{:S(2)}) async-start(s8[6291456]{0:T(1024)(128)(4,1)} %bitcast.236), calls=%async_computation.4 | async-start | bytes 8388608
  310.7 6.5 %slice-start.3 = ((s8[6291456]{0:T(1024)(128)(4,1)}), s8[2097152]{0:T(1024)(128)(4,1)S(1)}, s32[]{:S(2)}) async-start(s8[6291456]{0:T(1024)(128)(4,1)} %bitcast.236), calls=%async_computation.5 | async-start | bytes 4194304
  310.7 8.6 %copy-start.3 = (bf16[2,64,12,11,97]{4,3,1,2,0:T(8,128)(2,1)S(1)}, bf16[2,64,12,11,97]{4,3,1,2,0:T(8,128)(2,1)}, u32[]{:S(2)}) copy-start(bf16[2,64,12,11,97]{4,3,1,2,0:T(8,128)(2,1)} %reshape.194) | copy-start | bytes 9833476
  331.1 3.9 %copy-start.7 = (bf16[768,640]{1,0:T(8,128)(2,1)S(1)}, bf16[768,640]{1,0:T(8,128)(2,1)}, u32[]{:S(2)}) copy-start(bf16[768,640]{1,0:T(8,128)(2,1)} %copy.123) | copy-start | bytes 2949124
  368.6 12.5 %copy-start.1 = (bf16[6,5,31]{2,0,1:T(8,128)(2,1)S(1)}, bf16[6,5,31]{2,0,1:T(8,128)(2,1)}, u32[]{:S(2)}) copy-start(bf16[6,5,31]{2,0,1:T(8,128)(2,1)} %param.16) | copy-start | bytes 5584
where the time goes:
time: 387 us; the launch traced here: 381 us
  local copies, waits for them, and re-layouts  175 us (45%)
  other arithmetic  80.4 us (21%)
  matrix products  61.5 us (16%)
  waiting for transfers between devices  45.4 us (12%)
  starting transfers between devices  17.8 us (5%)
    unnamed x26, other arithmetic  58.8 us
    all_to_all x1, waiting for transfers between devices, per_device(): lax.all_to_all(picked, 'shot', split_axis=2, concat_axis=0, tiled=True)  45.4 us
    another operation x1, local copies, waits for them, and re-layouts, per_device(): stacked = jnp.stack(slab_list, axis=-2)  37.5 us
    dot_general x1, matrix products, per_device(): jnp.dot(stacked.reshape(-1, 5 * 128), recv_matrix, preferred_element_type...  28.7 us
    dot_general x1, matrix products, per_device(): jnp.dot(stacked.reshape(-1, 15 * 128), shot_matrix, preferred_element_typ...  27.1 us
    reshape x2, local copies, waits for them, and re-layouts, time_windows(): padded[..., stride:stride + total].reshape(lead + (num_blocks, stride))  20.2 us
    slice x3, local copies, waits for them, and re-layouts, time_windows(): head_part = padded[..., :total].reshape(lead + (num_blocks, stride))  19.5 us
    reshape x2, local copies, waits for them, and re-layouts, time_windows(): head_part = padded[..., :total].reshape(lead + (num_blocks, stride))  19.4 us
  transfers between devices with their start and end apart: 4, of which 1 were waited for; matrix products, arithmetic and copies ran while one was open for 51% of the time, Pallas kernels for 0%

commit v1 on v0

v1 whole, which is shorter than its diff:
```python
import functools

import jax
import jax.numpy as jnp
from jax import lax
from jax.experimental import pallas as pl
from jax.experimental.pallas import tpu as pltpu
from jax.sharding import PartitionSpec as P

BF = jnp.bfloat16
F32 = jnp.float32
STEP_ONE = 32
STEP_TWO = 16
VMEM = 58 * 1024 * 1024


def band_matrix(kernels, step, chunks):
    bank, taps = kernels.shape[0], kernels.shape[-1]
    flat = kernels.reshape(bank, -1, taps)
    out_pos = jnp.arange(step, dtype=jnp.int32)[:, None, None]
    in_pos = jnp.arange(step * chunks, dtype=jnp.int32)[None, :, None]
    tap = jnp.arange(taps, dtype=jnp.int32)[None, None, :]
    lead = 16 - taps // 2
    onehot = (in_pos - out_pos - lead == tap).astype(BF).reshape(step, chunks, step, taps)
    band = jnp.einsum("kot,ujrt->kujor", flat, onehot, preferred_element_type=F32)
    return band.astype(BF).reshape(bank * step, -1)


def nt_dot(a, b):
    return lax.dot_general(a, b, (((1,), (1,)), ((), ())), preferred_element_type=F32)


def shrink(filtered, tau_ref, bank, step):
    total = None
    for k in range(bank):
        f = filtered[k * step : (k + 1) * step]
        sq = f * f
        tau = tau_ref[k]
        term = (f * sq) * pl.reciprocal(sq + tau * tau, approx=True)
        total = term if total is None else total + term
    return total


def shot_kernel(live_ref, top_ref, bottom_ref, mask_ref, band_ref, tau_ref, row_ref, out_ref, wins, clean, pick):
    lines, channels, samples = live_ref.shape
    step = STEP_ONE
    blocks = samples // step
    bank = tau_ref.shape[0]
    depth = 5 * step
    src = lax.broadcasted_iota(jnp.int32, (channels, channels), 0)
    dst = lax.broadcasted_iota(jnp.int32, (channels, channels), 1)
    shifts = [jnp.where(src == dst + (b - 2), 1.0, 0.0).astype(BF) for b in range(5)]
    zeros = jnp.zeros((16, channels), BF)
    for n in range(lines + 2):
        for b in range(5):
            base = n * depth + b * step
            wins[0, base : base + 16, :] = zeros
            wins[blocks, base + 16 : base + 32, :] = zeros

    per = 128 // step
    for n in range(lines + 2):
        ref = top_ref.at[0] if n == 0 else bottom_ref.at[0] if n == lines + 1 else live_ref.at[n - 1]

        def spread(m, carry, n=n, ref=ref):
            cols = pl.ds(pl.multiple_of(m * 128, 128), 128)
            turned = ref[:, cols].astype(F32).T.astype(BF)
            for b in range(5):
                base = n * depth + b * step
                if b == 2:
                    moved = turned
                else:
                    moved = jnp.dot(turned, shifts[b], preferred_element_type=F32).astype(BF)
                wins[m * per, base + 16 : base + 32, :] = moved[0:16]
                for q in range(1, per):
                    wins[m * per + q, base : base + 32, :] = moved[q * 32 - 16 : q * 32 + 16]
                wins[m * per + per, base : base + 16, :] = moved[112:128]
            return carry

        lax.fori_loop(0, samples // 128, spread, 0)

    half = 3 * depth

    def block(j, carry):
        for n in range(lines):
            lo = n * depth
            filtered = jnp.dot(band_ref[:, :half], wins[j, lo : lo + half, :], preferred_element_type=F32)
            filtered += jnp.dot(band_ref[:, half:], wins[j + 1, lo : lo + half, :], preferred_element_type=F32)
            noise = shrink(filtered, tau_ref, bank, step)
            mid = lo + depth + 2 * step
            live = jnp.concatenate(
                [wins[j, mid + 16 : mid + 32, :].astype(F32), wins[j + 1, mid : mid + 16, :].astype(F32)], axis=0
            )
            kept = (live - noise) * mask_ref[n : n + 1, :]
            clean[pl.ds(pl.multiple_of(j * step, step), step), n * channels : (n + 1) * channels] = kept.astype(BF)
        return carry

    lax.fori_loop(0, blocks, block, 0)

    rows = out_ref.shape[0]
    spot = lax.broadcasted_iota(jnp.int32, (rows, lines * channels), 0)
    pick[...] = jnp.where(spot == row_ref[...], 1.0, 0.0).astype(BF)

    def route(m, carry):
        span = pl.ds(pl.multiple_of(m * 256, 256), 256)
        out_ref[:, span] = nt_dot(pick[...], clean[span, :]).astype(BF)
        return carry

    lax.fori_loop(0, samples // 256, route, 0)


def receiver_kernel(folds, got_ref, spot_ref, band_ref, tau_ref, out_ref, wins, done, place, perm):
    rows, samples = got_ref.shape
    width = spot_ref.shape[1]
    fold_lanes = width // folds
    step = STEP_TWO
    blocks = samples // step
    bank = tau_ref.shape[0]
    depth = 5 * step
    aligned = fold_lanes % 128 == 0
    wins[0] = jnp.zeros((depth, width), BF)
    wins[blocks + 1] = jnp.zeros((depth, width), BF)
    ids = lax.broadcasted_iota(jnp.int32, (rows, width), 0)
    for b in [2] if aligned else range(5):
        place[0 if aligned else b] = jnp.where(ids == spot_ref[b : b + 1, :], 1.0, 0.0).astype(BF)
    out_id = lax.broadcasted_iota(jnp.int32, (width, width), 0)
    lane = lax.broadcasted_iota(jnp.int32, (width, width), 1)
    perm[...] = jnp.where((out_id % folds) * fold_lanes + out_id // folds == lane, 1.0, 0.0).astype(BF)
    per = 128 // step

    def assemble(m, carry):
        cols = pl.ds(pl.multiple_of(m * 128, 128), 128)
        turned = got_ref[:, cols].astype(F32).T.astype(BF)
        at = pl.ds(m * per + 1, per)
        if aligned:
            cells = jnp.dot(turned, place[0], preferred_element_type=F32).astype(BF)
            cells = cells.reshape(per, step, width)
            for b in range(5):
                gap = (b - 2) * fold_lanes
                lo, hi = max(0, -gap), width - max(0, gap)
                r = slice(b * step, (b + 1) * step)
                wins[at, r, lo:hi] = cells[:, :, lo + gap : hi + gap]
                if lo > 0:
                    wins[at, r, 0:lo] = jnp.zeros((per, step, lo), BF)
                if hi < width:
                    wins[at, r, hi:width] = jnp.zeros((per, step, width - hi), BF)
        else:
            for b in range(5):
                cells = jnp.dot(turned, place[b], preferred_element_type=F32).astype(BF)
                wins[at, b * step : (b + 1) * step, :] = cells.reshape(per, step, width)
        return carry

    lax.fori_loop(0, samples // 128, assemble, 0)

    def block(j, carry):
        for g in range(width // 256):
            lanes = slice(g * 256, (g + 1) * 256)
            stack = wins[pl.ds(j, 3), :, lanes].reshape(3 * depth, 256)
            filtered = jnp.dot(band_ref[...], stack, preferred_element_type=F32)
            noise = shrink(filtered, tau_ref, bank, step)
            centre = wins[j + 1, 2 * step : 3 * step, lanes].astype(F32)
            mask = jnp.where(spot_ref[2:3, lanes] >= 0, 1.0, 0.0)
            done[pl.ds(pl.multiple_of(j * step, step), step), lanes] = ((centre - noise) * mask).astype(BF)
        return carry

    lax.fori_loop(0, blocks, block, 0)

    def restore(m, carry):
        span = pl.ds(pl.multiple_of(m * 256, 256), 256)
        turned = nt_dot(perm[...], done[span, :])
        out_ref[:, :, span] = turned.reshape(fold_lanes, folds, 256).astype(BF)
        return carry

    lax.fori_loop(0, samples // 256, restore, 0)


def vmem():
    return pl.BlockSpec(memory_space=pltpu.VMEM)


def smem():
    return pl.BlockSpec(memory_space=pltpu.SMEM)


def per_device(
    data, live_mask, patch_start, receiver_slot, shot_kernels, shot_tau, receiver_kernels, receiver_tau
):
    _, lines, channels, samples = data.shape
    stations = receiver_slot.shape[1]
    shots = patch_start.shape[0]
    owners = lax.axis_size("shot")
    slots = stations // owners
    me = lax.axis_index("shot")
    first_line = lax.axis_index("line") * lines
    ends = lax.axis_size("line") - 1
    fold_lanes = lines * slots
    width = shots * fold_lanes
    capacity = fold_lanes

    mask = live_mask[0]
    live = data[0] * mask[..., None].astype(BF)
    top = lax.ppermute(live[lines - 1 :], "line", [(i, i + 1) for i in range(ends)])
    bottom = lax.ppermute(live[:1], "line", [(i + 1, i) for i in range(ends)])

    band_one = band_matrix(shot_kernels, STEP_ONE, 2)
    band_two = band_matrix(receiver_kernels, STEP_TWO, 3)

    starts = lax.dynamic_slice_in_dim(patch_start, first_line, lines, 1)
    own_starts = lax.dynamic_slice_in_dim(starts, me, 1, 0)[0]
    own_slots = jnp.concatenate(
        [lax.dynamic_slice(receiver_slot, (n, own_starts[n]), (1, channels)) for n in range(lines)], axis=0
    )
    owner = own_slots // slots
    line_ids = jnp.arange(lines, dtype=jnp.int32)[:, None]
    rows = owner * capacity + line_ids * slots + own_slots % slots
    rows = rows.reshape(1, lines * channels)
    slot_ids = me * slots + jnp.arange(slots, dtype=jnp.int32)
    hits = receiver_slot[:, None, :] == slot_ids[None, :, None]
    station = jnp.sum(jnp.where(hits, jnp.arange(stations, dtype=jnp.int32), 0), axis=-1)
    channel = station[None] - starts[:, :, None]
    covered = (channel >= 0) & (channel < channels)
    covered = covered.reshape(shots, fold_lanes)
    before = jnp.tril(jnp.ones((shots, shots), jnp.int32), -1)
    fold = jnp.sum(before[:, :, None] * covered[None].astype(jnp.int32), axis=1)
    source = jnp.arange(shots, dtype=jnp.int32)[:, None] * capacity + jnp.arange(fold_lanes, dtype=jnp.int32)[None]
    fold_ids = jnp.arange(shots, dtype=jnp.int32)[:, None, None]
    spot = jnp.sum(jnp.where(covered[None] & (fold[None] == fold_ids), source[None] + 1, 0), axis=1) - 1
    spot = spot.reshape(width)
    padded = jnp.pad(spot, (2 * fold_lanes, 2 * fold_lanes), constant_values=-1)
    spots = jnp.stack([padded[b * fold_lanes : b * fold_lanes + width] for b in range(5)])

    blocks = samples // STEP_ONE
    send = pl.pallas_call(
        shot_kernel,
        out_shape=jax.ShapeDtypeStruct((owners * capacity, samples), BF),
        in_specs=[vmem(), vmem(), vmem(), vmem(), vmem(), smem(), vmem()],
        out_specs=vmem(),
        scratch_shapes=[
            pltpu.VMEM((blocks + 1, (lines + 2) * 5 * STEP_ONE, channels), BF),
            pltpu.VMEM((samples, lines * channels), BF),
            pltpu.VMEM((owners * capacity, lines * channels), BF),
        ],
        compiler_params=pltpu.CompilerParams(vmem_limit_bytes=VMEM),
        name="shot_bank",
    )(live, top, bottom, mask.astype(F32), band_one, shot_tau, rows)

    got = lax.all_to_all(send.reshape(owners, capacity, samples), "shot", split_axis=0, concat_axis=0, tiled=True)
    got = got.reshape(shots * capacity, samples)

    count = 1 if fold_lanes % 128 == 0 else 5
    out = pl.pallas_call(
        functools.partial(receiver_kernel, shots),
        out_shape=jax.ShapeDtypeStruct((fold_lanes, shots, samples), BF),
        in_specs=[vmem(), vmem(), vmem(), smem()],
        out_specs=vmem(),
        scratch_shapes=[
            pltpu.VMEM((samples // STEP_TWO + 2, 5 * STEP_TWO, width), BF),
            pltpu.VMEM((samples, width), BF),
            pltpu.VMEM((count, shots * capacity, width), BF),
            pltpu.VMEM((width, width), BF),
        ],
        compiler_params=pltpu.CompilerParams(vmem_limit_bytes=VMEM),
        name="receiver_bank",
    )(got, spots, band_two, receiver_tau)
    return out.reshape(lines, slots, shots, samples)


def solution(mesh):
    return jax.shard_map(
        per_device,
        mesh=mesh,
        in_specs=(
            P("shot", "line", None, None),
            P("shot", "line", None),
            P(),
            P("line", None),
            P(),
            P(),
            P(),
            P(),
        ),
        out_specs=P("line", "shot", None, None),
        check_vma=False,
    )
```

time: 387 us -> 133 us (0.34); the launches traced: 381 us -> 133 us
  local copies, waits for them, and re-layouts: 175 us -> 8.1 us
  other arithmetic: 80.4 us -> 3.83 us
  matrix products: 61.5 us -> 2 us
  Pallas kernels: 0 us -> 57.2 us
  starting transfers between devices: 17.8 us -> 11.1 us
    dot_general x5 -> x2, matrix products: 61.5 us -> 2 us  [band_matrix(): jnp.einsum('kot,ujrt->kujor', flat, onehot, preferred_element_type=F32)]
    unnamed x26 -> x1, other arithmetic: 58.8 us -> 0.01 us
    pallas_call x0 -> x2, Pallas kernels: none -> 57.2 us  [the longest x1 30 us: per_device(): pl.pallas_call(shot_kernel, out_shape=jax.ShapeDtypeStruct((owners * capa...]
    reshape x5 -> x3, local copies, waits for them, and re-layouts: 48.1 us -> 3.48 us  [band_matrix(): return band.astype(BF).reshape(bank * step, -1)]
    another operation x1, local copies, waits for them, and re-layouts: 37.5 us -> 0.64 us  [per_device(): jnp.stack([padded[b * fold_lanes:b * fold_lanes + width] for b in range(5)])]
    slice x8 -> x3, local copies, waits for them, and re-layouts: 34.6 us -> 1.75 us  [the longest x1 1.14 us: per_device(): bottom = lax.ppermute(live[:1], 'line', [(i + 1, i) for i in range(ends)])]
    gather x5 -> x0, local copies, waits for them, and re-layouts: 28.2 us -> none  [the longest x1 10 us: per_device(): picked = jnp.take_along_axis(cleaned, clipped[..., None], axis=2)]
    unnamed x57 -> x16, local copies, waits for them, and re-layouts: 18.3 us -> 1.46 us
  transfers between devices with their start and end apart: 4 -> 3, of which waited for: 1 -> 1; matrix products, arithmetic and copies ran while one was open for 51% -> 7% of each run, Pallas kernels for 0% -> 0%
where the time goes in v1:
time: 133 us
  Pallas kernels  57.2 us (43%)
  waiting for transfers between devices  46.5 us (35%)
  starting transfers between devices  11.1 us (8%)
  local copies, waits for them, and re-layouts  8.1 us (6%)
  between operations  4 us (3%)
  other arithmetic  3.83 us (3%)
  matrix products  2 us (2%)
    all_to_all x1, waiting for transfers between devices, per_device(): lax.all_to_all(send.reshape(owners, capacity, samples), 'shot', split_axi...  46.5 us
    pallas_call x1, Pallas kernels, per_device(): pl.pallas_call(shot_kernel, out_shape=jax.ShapeDtypeStruct((owners * capa...  30 us
    pallas_call x1, Pallas kernels, per_device(): pl.pallas_call(functools.partial(receiver_kernel, shots), out_shape=jax.S...  27.2 us
    all_to_all x1, starting transfers between devices, per_device(): lax.all_to_all(send.reshape(owners, capacity, samples), 'shot', split_axi...  6.63 us
    reshape x3, local copies, waits for them, and re-layouts, band_matrix(): return band.astype(BF).reshape(bank * step, -1)  3.48 us
    ppermute x1, starting transfers between devices, per_device(): lax.ppermute(live[lines - 1:], 'line', [(i, i + 1) for i in range(ends)])  3.16 us
  transfers between devices with their start and end apart: 3, of which 1 were waited for; matrix products, arithmetic and copies ran while one was open for 7% of the time, Pallas kernels for 0%

profile of v1, /device:TPU:0, one launch (start us, length us, event | category | flops | bytes accessed | tf_op | source)
XLA Modules:
  0.0 132.7 jit_solution(465330530206106579)
XLA Ops:
  0.0 0.0 copy-start
  0.0 1.3 %convert_bitcast_fusion = (f32[2,256]{1,0:T(2,128)}, bf16[2,256]{1,0:T(2,128)(2,1)S(1)}) fusion(s32[1,2,256]{2,1,0:T(2,128)} %param.9), kind=kLoop, calls=%fused_computation.37 | loop fusion | flops 1024 | bytes 5120 | tf_op jit(solution)/shard_map/convert_element_type | solution.py:244
  1.3 0.0 copy-start.3
  1.3 1.4 %bitcast_multiply_fusion.live_ref = bf16[2,256,1024]{2,1,0:T(8,128)(2,1)S(1)} fusion(bf16[1,2,256,1024]{3,2,1,0:T(8,128)(2,1)} %param.8, bf16[2,256]{1,0:T(2,128)(2,1)S(1)} %get-tuple-element.18), kind=kLoop, calls=%fused_computation.4 | loop fusion | flops 524288 | bytes 2098176 | tf_op jit(solution)/shard_map/mul | solution.py:200
  2.7 0.0 copy-start.1
  2.7 0.0 copy-start.5
  2.7 1.1 fusion.15
  3.9 3.2 %collective-permute-start = (bf16[1,256,1024]{2,1,0:T(8,128)(2,1)}, bf16[1,256,1024]{2,1,0:T(8,128)(2,1)}, u32[]{:S(2)}, u32[]{:S(2)}) collective-permute-start(bf16[1,256,1024]{2,1,0:T(8,128)(2,1)} %get-tuple-element.8), channel_id=1, source_target_pairs={{0,1},{1,2},{2,3},{4,5},{5,6},{6,7},{8,9},{9,10},{10,11},{12,13},{... | collective-permute-start | bytes 1572872 | tf_op jit(solution)/shard_map/ppermute | solution.py:201
  7.0 1.3 collective-permute-start.1
  8.4 0.0 copy-done.3
  8.4 0.1 broadcast_bitcast_fusion
  8.5 1.3 fusion
  9.8 0.0 copy-done.1
  9.8 0.0 copy-done.5
  9.8 0.1 dynamic_slice.12
  9.9 0.6 fusion.16
  13.0 0.0 copy-start.4
  13.0 0.3 copy.18
  13.3 2.5 %reshape.308.band_ref = bf16[192,960]{1,0:T(8,128)(2,1)} reshape(bf16[6,32,2,15,32]{4,3,2,1,0:T(8,128)(2,1)S(1)} %copy.18) | data formatting | bytes 737280 | tf_op jit(solution)/shard_map/reshape | solution.py:26
  17.1 0.0 copy-done.4
  17.1 0.1 constant_dynamic-slice_fusion.1
  17.2 0.6 fusion.12.row_ref
  17.8 0.0 collective-permute-done.top_ref
  17.8 0.0 collective-permute-done.1.bottom_ref
  17.8 30.0 %shot_bank.1 = bf16[1024,1024]{1,0:T(8,128)(2,1)} custom-call(bf16[2,256,1024]{2,1,0:T(8,128)(2,1)} %copy-done.1, bf16[1,256,1024]{2,1,0:T(8,128)(2,1)} %collective-permute-done.top_ref, bf16[1,256,1024]{2,1,0:T(8,128)(2,1)} %collective-permute-done.1.bottom_ref, f32[2,256]{1,0:T(2,128)} %get-tuple-element.17.mask_ref, bf16[192,960]{1,0:T(8,128)(2,1)} %reshape.308.band_ref, ...), custom_call_target="tpu_custom_call" | custom-call | tf_op jit(solution)/shard_map/shot_bank/pallas_call | solution.py:232
  47.8 6.6 %all-to-all-start = ((bf16[8,128,1024]{2,1,0:T(8,128)(2,1)}), bf16[8,128,1024]{2,1,0:T(8,128)(2,1)S(1)}, u32[]{:S(2)}, u32[]{:S(2)}) async-start(bf16[8,128,1024]{2,1,0:T(8,128)(2,1)} %bitcast.48), calls=%async_computation | async-start | bytes 4194304 | tf_op jit(solution)/shard_map/all_to_all | solution.py:246
  54.4 0.1 constant_dynamic-slice_fusion
  54.5 0.1 sub.115
  54.5 0.1 sub.116
  54.6 0.2 select_reduce_fusion
  54.8 0.1 sub.113
  54.9 0.0 copy-done
  54.9 0.7 fusion.1
  55.7 0.1 copy.27
  55.8 0.9 reshape.317.band_ref
  56.7 0.1 fusion.11
  56.8 0.1 multiply_reduce_fusion
  56.9 0.1 add_add_fusion
  57.0 0.6 stack.20.spot_ref
  57.6 46.5 %all-to-all-done = bf16[8,128,1024]{2,1,0:T(8,128)(2,1)S(1)} async-done(((bf16[8,128,1024]{2,1,0:T(8,128)(2,1)}), bf16[8,128,1024]{2,1,0:T(8,128)(2,1)S(1)}, u32[]{:S(2)}, u32[]{:S(2)}) %all-to-all-start) | async-done | bytes 2097184 | tf_op jit(solution)/shard_map/all_to_all | solution.py:246
  104.1 0.0 copy-start.2
  104.2 1.3 %copy-done.2 = bf16[8,128,1024]{2,1,0:T(8,128)(2,1)} copy-done((bf16[8,128,1024]{2,1,0:T(8,128)(2,1)}, bf16[8,128,1024]{2,1,0:T(8,128)(2,1)S(1)}, u32[]{:S(2)}) %copy-start.2) | copy-done | bytes 2097176
  105.5 27.2 %receiver_bank.1 = bf16[128,8,1024]{2,1,0:T(8,128)(2,1)} custom-call(bf16[1024,1024]{1,0:T(8,128)(2,1)} %bitcast.49, s32[5,1024]{1,0:T(8,128)} %stack.20.spot_ref, bf16[96,240]{1,0:T(8,128)(2,1)} %reshape.317.band_ref, f32[6]{0:T(128)} %tau_ref.3), custom_call_target="tpu_custom_call" | custom-call | tf_op jit(solution)/shard_map/receiver_bank/pallas_call | solution.py:250
  (16 shorter events, 0.1 us)
Async XLA Ops:
  0.0 54.9 %copy-start = (bf16[6,5,31]{2,0,1:T(8,128)(2,1)S(1)}, bf16[6,5,31]{2,0,1:T(8,128)(2,1)}, u32[]{:S(2)}) copy-start(bf16[6,5,31]{2,0,1:T(8,128)(2,1)} %param.14) | copy-start | bytes 5584
  1.3 7.0 %copy-start.3 = (bf16[6,3,5,31]{3,1,2,0:T(4,128)(2,1)S(1)}, bf16[6,3,5,31]{3,1,2,0:T(4,128)(2,1)}, u32[]{:S(2)}) copy-start(bf16[6,3,5,31]{3,1,2,0:T(4,128)(2,1)} %param.12) | copy-start | bytes 16744
  2.7 7.0 %copy-start.1 = (bf16[2,256,1024]{2,1,0:T(8,128)(2,1)}, bf16[2,256,1024]{2,1,0:T(8,128)(2,1)S(1)}, u32[]{:S(2)}) copy-start(bf16[2,256,1024]{2,1,0:T(8,128)(2,1)S(1)} %bitcast_multiply_fusion.live_ref) | copy-start | bytes 3145732
  2.7 7.1 %copy-start.5 = (s32[8,8]{1,0:T(8,128)S(1)}, s32[8,8]{1,0:T(8,128)}, u32[]{:S(2)}) copy-start(s32[8,8]{1,0:T(8,128)} %param.10) | copy-start | bytes 772
  3.9 13.9 %collective-permute-start = (bf16[1,256,1024]{2,1,0:T(8,128)(2,1)}, bf16[1,256,1024]{2,1,0:T(8,128)(2,1)}, u32[]{:S(2)}, u32[]{:S(2)}) collective-permute-start(bf16[1,256,1024]{2,1,0:T(8,128)(2,1)} %get-tuple-element.8), channel_id=1, source_target_pairs={{0,1},{1,2},{2,3},{4,5},{5,6},{6,7},{8,9},{9,10},{10,11},{12,13},{... | collective-permute-start | bytes 1572872 | tf_op jit(solution)/shard_map/ppermute | solution.py:201
  7.0 10.8 %collective-permute-start.1 = (bf16[1,256,1024]{2,1,0:T(8,128)(2,1)}, bf16[1,256,1024]{2,1,0:T(8,128)(2,1)}, u32[]{:S(2)}, u32[]{:S(2)}) collective-permute-start(bf16[1,256,1024]{2,1,0:T(8,128)(2,1)} %get-tuple-element.7), channel_id=1, source_target_pairs={{1,0},{2,1},{3,2},{5,4},{6,5},{7,6},{9,8},{10,9},{11,10},{13,12},{... | collective-permute-start | bytes 1572872 | tf_op jit(solution)/shard_map/ppermute | solution.py:202
  13.0 4.1 %copy-start.4 = (s32[2,512]{1,0:T(2,128)S(1)}, s32[2,512]{1,0:T(2,128)}, u32[]{:S(2)}) copy-start(s32[2,512]{1,0:T(2,128)} %param.11) | copy-start | bytes 12292
  47.8 56.4 %all-to-all-start = ((bf16[8,128,1024]{2,1,0:T(8,128)(2,1)}), bf16[8,128,1024]{2,1,0:T(8,128)(2,1)S(1)}, u32[]{:S(2)}, u32[]{:S(2)}) async-start(bf16[8,128,1024]{2,1,0:T(8,128)(2,1)} %bitcast.48), calls=%async_computation | async-start | bytes 4194304 | tf_op jit(solution)/shard_map/all_to_all | solution.py:246
  104.1 1.3 %copy-start.2 = (bf16[8,128,1024]{2,1,0:T(8,128)(2,1)}, bf16[8,128,1024]{2,1,0:T(8,128)(2,1)S(1)}, u32[]{:S(2)}) copy-start(bf16[8,128,1024]{2,1,0:T(8,128)(2,1)S(1)} %all-to-all-done) | copy-start | bytes 6291460

commit v2 on v1

v2 whole, which is shorter than its diff:
```python
import functools
import math

import jax
import jax.numpy as jnp
from jax import lax
from jax.experimental import pallas as pl
from jax.experimental.pallas import tpu as pltpu
from jax.sharding import PartitionSpec as P

BF = jnp.bfloat16
F32 = jnp.float32
STEP_ONE = 32
STEP_TWO = 16
CHUNKS = 4
VMEM = 58 * 1024 * 1024


def band_matrix(kernels, step, chunks):
    bank, taps = kernels.shape[0], kernels.shape[-1]
    flat = kernels.reshape(bank, -1, taps)
    out_pos = jnp.arange(step, dtype=jnp.int32)[:, None, None]
    in_pos = jnp.arange(step * chunks, dtype=jnp.int32)[None, :, None]
    tap = jnp.arange(taps, dtype=jnp.int32)[None, None, :]
    lead = 16 - taps // 2
    onehot = (in_pos - out_pos - lead == tap).astype(BF).reshape(step, chunks, step, taps)
    band = jnp.einsum("kot,ujrt->kujor", flat, onehot, preferred_element_type=F32)
    return band.astype(BF).reshape(bank * step, -1)


def nt_dot(a, b):
    return lax.dot_general(a, b, (((1,), (1,)), ((), ())), preferred_element_type=F32)


def shrink(filtered, tau_ref, bank, step):
    total = None
    for k in range(bank):
        f = filtered[k * step : (k + 1) * step]
        sq = f * f
        tau = tau_ref[k]
        term = (f * sq) * pl.reciprocal(sq + tau * tau, approx=True)
        total = term if total is None else total + term
    return total


def bank_kernel(
    folds, live_ref, top_ref, bottom_ref, mask_ref, row_ref, spot_ref, band_one, tau_one, band_two, tau_two,
    out_ref, wins, clean, pick, send, recv, cells_win, done, place, perm, send_sem, recv_sem,
):
    lines, channels, samples = live_ref.shape
    chunks, rows, span = send.shape
    owners = lax.axis_size("shot")
    me = lax.axis_index("shot")
    capacity = rows // owners
    width = spot_ref.shape[1]
    fold_lanes = width // folds
    aligned = fold_lanes % 128 == 0

    barrier = pltpu.get_barrier_semaphore()
    for k in range(1, owners):
        pl.semaphore_signal(
            barrier, inc=1, device_id={"shot": lax.rem(me + k, owners)}, device_id_type=pl.DeviceIdType.MESH
        )

    step = STEP_ONE
    blocks = samples // step
    bank = tau_one.shape[0]
    depth = 5 * step
    half = 3 * depth
    per = 128 // step
    tiles = span // 128
    src = lax.broadcasted_iota(jnp.int32, (channels, channels), 0)
    dst = lax.broadcasted_iota(jnp.int32, (channels, channels), 1)
    shifts = [jnp.where(src == dst + (b - 2), 1.0, 0.0).astype(BF) for b in range(5)]
    zeros = jnp.zeros((16, channels), BF)
    for n in range(lines + 2):
        for b in range(5):
            base = n * depth + b * step
            wins[0, base : base + 16, :] = zeros
            wins[blocks, base + 16 : base + 32, :] = zeros
    spot = lax.broadcasted_iota(jnp.int32, (rows, lines * channels), 0)
    pick[...] = jnp.where(spot == row_ref[...], 1.0, 0.0).astype(BF)

    def spread(m, carry):
        cols = pl.ds(pl.multiple_of(m * 128, 128), 128)
        for n in range(lines + 2):
            ref = top_ref.at[0] if n == 0 else bottom_ref.at[0] if n == lines + 1 else live_ref.at[n - 1]
            turned = ref[:, cols].astype(F32).T.astype(BF)
            for b in range(5):
                base = n * depth + b * step
                if b == 2:
                    moved = turned
                else:
                    moved = jnp.dot(turned, shifts[b], preferred_element_type=F32).astype(BF)
                wins[m * per, base + 16 : base + 32, :] = moved[0:16]
                for q in range(1, per):
                    wins[m * per + q, base : base + 32, :] = moved[q * 32 - 16 : q * 32 + 16]
                wins[m * per + per, base : base + 16, :] = moved[112:128]
        return carry

    def block_one(j, carry):
        for n in range(lines):
            lo = n * depth
            filtered = jnp.dot(band_one[:, :half], wins[j, lo : lo + half, :], preferred_element_type=F32)
            filtered += jnp.dot(band_one[:, half:], wins[j + 1, lo : lo + half, :], preferred_element_type=F32)
            noise = shrink(filtered, tau_one, bank, step)
            mid = lo + depth + 2 * step
            live = jnp.concatenate(
                [wins[j, mid + 16 : mid + 32, :].astype(F32), wins[j + 1, mid : mid + 16, :].astype(F32)], axis=0
            )
            kept = (live - noise) * mask_ref[n : n + 1, :]
            clean[pl.ds(pl.multiple_of(j * step, step), step), n * channels : (n + 1) * channels] = kept.astype(BF)
        return carry

    def copy(i, k):
        to = lax.rem(me + k, owners)
        return pltpu.make_async_remote_copy(
            src_ref=send.at[i, pl.ds(pl.multiple_of(to * capacity, 16), capacity), :],
            dst_ref=recv.at[i, pl.ds(pl.multiple_of(me * capacity, 16), capacity), :],
            send_sem=send_sem.at[i, k],
            recv_sem=recv_sem.at[i, k],
            device_id={"shot": to},
            device_id_type=pl.DeviceIdType.MESH,
        )

    def chunk_one(i, carry):
        later = (i + chunks - 1) // chunks
        last = i // (chunks - 1)
        lax.fori_loop(tiles * i + later, tiles * (i + 1) + 1 - last, spread, 0)
        lax.fori_loop(i * (span // step), (i + 1) * (span // step), block_one, 0)
        at = pl.ds(pl.multiple_of(i * span, span), span)
        send[i] = nt_dot(pick[...], clean[at, :]).astype(BF)
        for k in range(1, owners):
            copy(i, k).start()
        own = pl.ds(pl.multiple_of(me * capacity, 16), capacity)
        recv[i, own, :] = send[i, own, :]
        return carry

    pl.semaphore_wait(barrier, owners - 1)
    lax.fori_loop(0, chunks, chunk_one, 0)

    step_two = STEP_TWO
    blocks_two = samples // step_two
    bank_two = tau_two.shape[0]
    depth_two = 5 * step_two
    cells_win[0] = jnp.zeros((depth_two, width), BF)
    cells_win[blocks_two + 1] = jnp.zeros((depth_two, width), BF)
    ids = lax.broadcasted_iota(jnp.int32, (rows, width), 0)
    for b in [2] if aligned else range(5):
        place[0 if aligned else b] = jnp.where(ids == spot_ref[b : b + 1, :], 1.0, 0.0).astype(BF)
    out_id = lax.broadcasted_iota(jnp.int32, (width, width), 0)
    lane = lax.broadcasted_iota(jnp.int32, (width, width), 1)
    perm[...] = jnp.where((out_id % folds) * fold_lanes + out_id // folds == lane, 1.0, 0.0).astype(BF)
    per_two = 128 // step_two

    def assemble(i, tile):
        turned = recv[i, :, tile * 128 : (tile + 1) * 128].astype(F32).T.astype(BF)
        at = pl.ds((i * tiles + tile) * per_two + 1, per_two)
        if aligned:
            cells = jnp.dot(turned, place[0], preferred_element_type=F32).astype(BF)
            cells = cells.reshape(per_two, step_two, width)
            for b in range(5):
                gap = (b - 2) * fold_lanes
                lo, hi = max(0, -gap), width - max(0, gap)
                r = slice(b * step_two, (b + 1) * step_two)
                cells_win[at, r, lo:hi] = cells[:, :, lo + gap : hi + gap]
                if lo > 0:
                    cells_win[at, r, 0:lo] = jnp.zeros((per_two, step_two, lo), BF)
                if hi < width:
                    cells_win[at, r, hi:width] = jnp.zeros((per_two, step_two, width - hi), BF)
        else:
            for b in range(5):
                cells = jnp.dot(turned, place[b], preferred_element_type=F32).astype(BF)
                cells_win[at, b * step_two : (b + 1) * step_two, :] = cells.reshape(per_two, step_two, width)

    def block_two(j, carry):
        for g in range(width // 256):
            lanes = slice(g * 256, (g + 1) * 256)
            stack = cells_win[pl.ds(j, 3), :, lanes].reshape(3 * depth_two, 256)
            filtered = jnp.dot(band_two[...], stack, preferred_element_type=F32)
            noise = shrink(filtered, tau_two, bank_two, step_two)
            centre = cells_win[j + 1, 2 * step_two : 3 * step_two, lanes].astype(F32)
            mask = jnp.where(spot_ref[2:3, lanes] >= 0, 1.0, 0.0)
            at = pl.ds(pl.multiple_of(j * step_two, step_two), step_two)
            done[at, lanes] = ((centre - noise) * mask).astype(BF)
        return carry

    def restore(m, carry):
        at = pl.ds(pl.multiple_of(m * 128, 128), 128)
        turned = nt_dot(perm[...], done[at, :])
        out_ref[:, :, at] = turned.reshape(fold_lanes, folds, 128).astype(BF)
        return carry

    def chunk_two(i, carry):
        later = (i + chunks - 1) // chunks
        last = i // (chunks - 1)
        for k in range(1, owners):
            copy(i, k).wait_recv()
        for tile in range(tiles):
            assemble(i, tile)
        count = span // step_two
        lax.fori_loop(i * count - later, (i + 1) * count - 1 + last, block_two, 0)
        lax.fori_loop(i * tiles - later, (i + 1) * tiles - 1 + last, restore, 0)
        return carry

    lax.fori_loop(0, chunks, chunk_two, 0)

    def finish(i, carry):
        for k in range(1, owners):
            copy(i, k).wait_send()
        return carry

    lax.fori_loop(0, chunks, finish, 0)


def packed_rows(lines, slots, channels, stations):
    share = channels / stations
    room = 5.5 * math.sqrt(lines * slots * share * (1 - share))
    return min(lines * slots, -(-int(lines * slots * share + room) // 16) * 16)


def vmem():
    return pl.BlockSpec(memory_space=pltpu.VMEM)


def smem():
    return pl.BlockSpec(memory_space=pltpu.SMEM)


def per_device(
    data, live_mask, patch_start, receiver_slot, shot_kernels, shot_tau, receiver_kernels, receiver_tau
):
    _, lines, channels, samples = data.shape
    stations = receiver_slot.shape[1]
    shots = patch_start.shape[0]
    owners = lax.axis_size("shot")
    slots = stations // owners
    me = lax.axis_index("shot")
    first_line = lax.axis_index("line") * lines
    ends = lax.axis_size("line") - 1
    fold_lanes = lines * slots
    width = shots * fold_lanes
    capacity = packed_rows(lines, slots, channels, stations)

    mask = live_mask[0]
    live = data[0] * mask[..., None].astype(BF)
    top = lax.ppermute(live[lines - 1 :], "line", [(i, i + 1) for i in range(ends)])
    bottom = lax.ppermute(live[:1], "line", [(i + 1, i) for i in range(ends)])

    starts = lax.dynamic_slice_in_dim(patch_start, first_line, lines, 1)
    own_starts = lax.dynamic_slice_in_dim(starts, me, 1, 0)[0]
    own_slots = jnp.concatenate(
        [lax.dynamic_slice(receiver_slot, (n, own_starts[n]), (1, channels)) for n in range(lines)], axis=0
    )
    owner = (own_slots // slots).reshape(-1)
    line_ids = jnp.arange(lines, dtype=jnp.int32)[:, None]
    place = (line_ids * slots + own_slots % slots).reshape(-1)
    ahead = (owner[:, None] == owner[None, :]) & (place[None, :] < place[:, None])
    rank = jnp.sum(ahead.astype(jnp.int32), axis=1)
    slot_ids = me * slots + jnp.arange(slots, dtype=jnp.int32)
    hits = receiver_slot[:, None, :] == slot_ids[None, :, None]
    station = jnp.sum(jnp.where(hits, jnp.arange(stations, dtype=jnp.int32), 0), axis=-1)
    channel = station[None] - starts[:, :, None]
    covered = (channel >= 0) & (channel < channels)
    covered = covered.reshape(shots, fold_lanes)
    lower = jnp.tril(jnp.ones((shots, shots), jnp.int32), -1)
    fold = jnp.sum(lower[:, :, None] * covered[None].astype(jnp.int32), axis=1)
    before = jnp.tril(jnp.ones((fold_lanes, fold_lanes), jnp.int32), -1)
    order = jnp.sum(before[None] * covered[:, None, :].astype(jnp.int32), axis=2)
    fold_ids = jnp.arange(shots, dtype=jnp.int32)[:, None, None]
    takes = covered[None] & (fold[None] == fold_ids)
    shot_ids = jnp.arange(shots, dtype=jnp.int32)[:, None]

    band_one = band_matrix(shot_kernels, STEP_ONE, 2)
    band_two = band_matrix(receiver_kernels, STEP_TWO, 3)
    blocks = samples // STEP_ONE
    copies = 1 if fold_lanes % 128 == 0 else 5
    weights = mask.astype(F32)

    def run(size, ident):
        rows = jnp.where(rank < size, owner * size + rank, -1).reshape(1, lines * channels)
        source = shot_ids * size + order
        spot = (jnp.sum(jnp.where(takes, source[None] + 1, 0), axis=1) - 1).reshape(width)
        padded = jnp.pad(spot, (2 * fold_lanes, 2 * fold_lanes), constant_values=-1)
        spots = jnp.stack([padded[b * fold_lanes : b * fold_lanes + width] for b in range(5)])
        total = owners * size
        return pl.pallas_call(
            functools.partial(bank_kernel, shots),
            out_shape=jax.ShapeDtypeStruct((fold_lanes, shots, samples), BF),
            in_specs=[vmem()] * 7 + [smem(), vmem(), smem()],
            out_specs=vmem(),
            scratch_shapes=[
                pltpu.VMEM((blocks + 1, (lines + 2) * 5 * STEP_ONE, channels), BF),
                pltpu.VMEM((samples, lines * channels), BF),
                pltpu.VMEM((total, lines * channels), BF),
                pltpu.VMEM((CHUNKS, total, samples // CHUNKS), BF),
                pltpu.VMEM((CHUNKS, total, samples // CHUNKS), BF),
                pltpu.VMEM((samples // STEP_TWO + 2, 5 * STEP_TWO, width), BF),
                pltpu.VMEM((samples, width), BF),
                pltpu.VMEM((copies, total, width), BF),
                pltpu.VMEM((width, width), BF),
                pltpu.SemaphoreType.DMA((CHUNKS, owners)),
                pltpu.SemaphoreType.DMA((CHUNKS, owners)),
            ],
            compiler_params=pltpu.CompilerParams(
                vmem_limit_bytes=VMEM, collective_id=ident, has_side_effects=True
            ),
            name="banks",
        )(live, top, bottom, weights, rows, spots, band_one, shot_tau, band_two, receiver_tau)

    if capacity == fold_lanes:
        out = run(fold_lanes, 0)
    else:
        all_channels = jnp.arange(stations, dtype=jnp.int32)[None, None, :] - starts[:, :, None]
        lit = (all_channels >= 0) & (all_channels < channels)
        of_owner = receiver_slot[None] // slots == jnp.arange(owners, dtype=jnp.int32)[:, None, None]
        most = jnp.max(jnp.sum((lit[:, None] & of_owner[None]).astype(jnp.int32), axis=(2, 3)))
        most = lax.pmax(most, "line")
        out = lax.cond(most > capacity, lambda: run(fold_lanes, 0), lambda: run(capacity, 1))
    return out.reshape(lines, slots, shots, samples)


def solution(mesh):
    return jax.shard_map(
        per_device,
        mesh=mesh,
        in_specs=(
            P("shot", "line", None, None),
            P("shot", "line", None),
            P(),
            P("line", None),
            P(),
            P(),
            P(),
            P(),
        ),
        out_specs=P("line", "shot", None, None),
        check_vma=False,
    )
```

time: 133 us -> 93.9 us (0.71)
  the two profiles are of different devices: /device:TPU:0 before, /device:TPU:26 now
where the time goes in v2:
time: 93.9 us; the launch traced here: 93.5 us
  Pallas kernels  57.6 us (61%)
  local copies, waits for them, and re-layouts  11.6 us (12%)
  blocking collectives  5.58 us (6%)
  other arithmetic  5.43 us (6%)
  between operations  4.96 us (5%)
  starting transfers between devices  4.34 us (5%)
  matrix products  3.69 us (4%)
    pallas_call x1, Pallas kernels, run(): pl.pallas_call(functools.partial(bank_kernel, shots), out_shape=jax.Shape...  57.6 us
    reshape x3, local copies, waits for them, and re-layouts, band_matrix(): return band.astype(BF).reshape(bank * step, -1)  5.59 us
    pmax x1, blocking collectives, per_device(): most = lax.pmax(most, 'line')  5.58 us
    dot_general x2, matrix products, band_matrix(): jnp.einsum('kot,ujrt->kujor', flat, onehot, preferred_element_type=F32)  3.69 us
    ppermute x1, starting transfers between devices, per_device(): lax.ppermute(live[lines - 1:], 'line', [(i, i + 1) for i in range(ends)])  3.06 us
  transfers between devices with their start and end apart: 2, of which 0 were waited for; matrix products, arithmetic and copies ran while one was open for 7% of the time, Pallas kernels for 0%

profile of v2, /device:TPU:26, one launch (start us, length us, event | category | flops | bytes accessed | tf_op | source)
XLA Modules:
  0.0 93.5 jit_solution(7491625753291514045)
XLA Ops:
  0.0 0.0 copy-start
  0.0 0.7 convert_bitcast_fusion.2
  0.7 1.4 %bitcast_multiply_fusion = bf16[2,256,1024]{2,1,0:T(8,128)(2,1)S(1)} fusion(bf16[1,2,256,1024]{3,2,1,0:T(8,128)(2,1)} %param.10, bf16[2,256]{1,0:T(2,128)(2,1)S(1)} %convert_bitcast_fusion.2), kind=kLoop, calls=%fused_computation.52 | loop fusion | flops 524288 | bytes 2098176 | tf_op jit(solution)/shard_map/mul | solution.py:246
  2.1 0.0 copy-start.7
  2.1 1.1 %fusion.27 = (bf16[1,256,1024]{2,1,0:T(8,128)(2,1)}, bf16[1,256,1024]{2,1,0:T(8,128)(2,1)}) fusion(bf16[2,256,1024]{2,1,0:T(8,128)(2,1)S(1)} %bitcast_multiply_fusion), kind=kLoop, calls=%fused_computation.96 | loop fusion | bytes 2097152 | tf_op jit(solution)/shard_map/slice | solution.py:248
  3.2 1.3 %collective-permute-start.1 = (bf16[1,256,1024]{2,1,0:T(8,128)(2,1)}, bf16[1,256,1024]{2,1,0:T(8,128)(2,1)S(1)}, u32[]{:S(2)}, u32[]{:S(2)}) collective-permute-start(bf16[1,256,1024]{2,1,0:T(8,128)(2,1)} %get-tuple-element.548), channel_id=1, source_target_pairs={{1,0},{2,1},{3,2},{5,4},{6,5},{7,6},{9,8},{10,9},{11,10},{13,12},{... | collective-permute-start | bytes 1572872 | tf_op jit(solution)/shard_map/ppermute | solution.py:248
  4.5 3.1 %collective-permute-start = (bf16[1,256,1024]{2,1,0:T(8,128)(2,1)}, bf16[1,256,1024]{2,1,0:T(8,128)(2,1)S(1)}, u32[]{:S(2)}, u32[]{:S(2)}) collective-permute-start(bf16[1,256,1024]{2,1,0:T(8,128)(2,1)} %get-tuple-element.549), channel_id=1, source_target_pairs={{0,1},{1,2},{2,3},{4,5},{5,6},{6,7},{8,9},{9,10},{10,11},{12,13},{... | collective-permute-start | bytes 1572872 | tf_op jit(solution)/shard_map/ppermute | solution.py:247
  7.6 0.0 copy-done.10
  7.6 0.1 dynamic_slice.13
  7.6 0.7 fusion.28
  11.0 0.1 constant_dynamic-slice_fusion.1
  11.1 0.1 sub.161
  11.2 0.1 sub.165
  11.2 0.1 sub.162
  11.3 0.1 compare_and_fusion
  11.4 0.0 copy-done.8
  11.5 0.2 select_reduce_fusion.2
  11.7 0.1 sub.159
  13.1 0.1 constant_dynamic-slice_fusion
  13.2 0.1 broadcast_bitcast_fusion
  13.4 0.2 convert_reduce_fusion
  13.6 0.6 reduce_max.9
  14.2 0.0 copy-done
  14.3 1.5 %fusion.13 = bf16[6,16,3,5,16]{4,0,3,2,1:T(8,128)(2,1)} fusion(s32[16,3,16]{2,1,0:T(4,128)S(1)} %subtract_add_fusion, bf16[6,5,31]{2,0,1:T(8,128)(2,1)S(1)} %copy-done), kind=kOutput, calls=%fused_computation.51 | convolution fusion | flops 1475328 | bytes 51012 | tf_op jit(solution)/shard_map/kot,ujrt->kujor/dot_general | solution.py:27
  15.8 5.6 %pmax.7 = s32[]{:T(128)} all-reduce(s32[]{:T(128)} %reduce_max.9), channel_id=1, replica_groups=mesh['shot'=8,'line'=4] {'line'}, use_global_device_ids=true, to_apply=%region_2.3 | all-reduce | flops 1 | bytes 8 | tf_op jit(solution)/shard_map/pmax | solution.py:318
  22.0 0.0 copy-done.7
  22.0 0.2 and_convert_fusion
  22.3 2.2 %fusion.12 = bf16[6,32,2,15,32]{4,3,0,2,1:T(8,128)(2,1)} fusion(s32[32,2,32]{2,1,0:T(2,128)S(1)} %subtract_add_fusion.1, bf16[6,15,31,1,1]{2,0,1,4,3:T(8,128)(2,1)S(1)} %bitcast.84), kind=kOutput, calls=%fused_computation.49 | convolution fusion | flops 11675648 | bytes 382412 | tf_op jit(solution)/shard_map/kot,ujrt->kujor/dot_general | solution.py:27
  24.4 0.0 collective-permute-done.1
  24.4 0.0 collective-permute-done
  24.5 67.7 %conditional.1 = (bf16[2,64,8,1024]{3,2,1,0:T(8,128)(2,1)S(1)}) conditional(s32[]{:T(128)} %convert_element_type.72, (s32[1,2,256]{2,1,0:T(2,128)S(1)}, s32[512,512]{1,0:T(8,128)S(1)}, s32[512]{0:T(512)S(1)}, s32[512]{0:T(512)S(1)}, pred[512]{0:T(512)(128)(4,1)S(1)}, /*index=5*/s32[512]{0:T(512)S(1)}, s32[512]{0:T(512)S(1)}, ...), branch_computations={%region_4.9_spmd, %region_9.14_spmd} | conditional | flops 612624 | bytes 8738848 | solution.py:319
  24.6 0.1 select_bitcast_fusion
  24.7 0.2 multiply_reduce_fusion
  24.9 0.1 add_add_fusion
  25.0 0.1 select_bitcast_fusion.1
  25.0 0.1 multiply_reduce_fusion.1
  25.1 0.2 copy-done.3
  25.3 0.1 reduce_sum.82
  25.5 0.0 copy-start.1
  25.5 0.6 fusion.3
  26.1 0.6 convert_bitcast_fusion.mask_ref
  26.7 0.7 stack.34.spot_ref
  27.3 1.1 %copy.35 = bf16[6,16,3,5,16]{4,3,2,1,0:T(8,128)(2,1)S(1)} copy(bf16[6,16,3,5,16]{4,0,3,2,1:T(8,128)(2,1)} %get-tuple-element.505) | data formatting | bytes 92160 | tf_op jit(solution)/shard_map/reshape | solution.py:28
  28.5 0.9 reshape.433.band_two
  29.4 1.5 %copy.27 = bf16[6,32,2,15,32]{4,3,2,1,0:T(8,128)(2,1)} copy(bf16[6,32,2,15,32]{4,3,0,2,1:T(8,128)(2,1)S(1)} %copy-done.1) | data formatting | bytes 737280 | tf_op jit(solution)/shard_map
  30.8 3.6 %reshape.420.band_one = bf16[192,960]{1,0:T(8,128)(2,1)} reshape(bf16[6,32,2,15,32]{4,3,2,1,0:T(8,128)(2,1)} %copy.27) | data formatting | bytes 737280 | tf_op jit(solution)/shard_map/reshape | solution.py:28
  34.4 57.6 %banks.4 = bf16[128,8,1024]{2,1,0:T(8,128)(2,1)S(1)} custom-call(bf16[2,256,1024]{2,1,0:T(8,128)(2,1)S(1)} %get-tuple-element.349.live_ref, bf16[1,256,1024]{2,1,0:T(8,128)(2,1)} %copy-done.5, bf16[1,256,1024]{2,1,0:T(8,128)(2,1)} %copy-done.3, f32[2,256]{1,0:T(2,128)} %convert_bitcast_fusion.mask_ref, s32[1,512]{1,0:T(1,128)} %bitcast.97, ...), custom_call_target="tpu_custom_call" | custom-call | tf_op jit(solution)/shard_map/cond/branch_0_fun/banks/pallas_call | solution.py:287
  92.2 1.3 %copy.48 = bf16[2,64,8,1024]{3,2,1,0:T(8,128)(2,1)} copy(bf16[2,64,8,1024]{3,2,1,0:T(8,128)(2,1)S(1)} %get-tuple-element.395) | data formatting | bytes 4194304
  (41 shorter events, 0.2 us)
Async XLA Ops:
  0.0 14.2 %copy-start = (bf16[6,5,31]{2,0,1:T(8,128)(2,1)S(1)}, bf16[6,5,31]{2,0,1:T(8,128)(2,1)}, u32[]{:S(2)}) copy-start(bf16[6,5,31]{2,0,1:T(8,128)(2,1)} %param.16) | copy-start | bytes 5584
  0.7 6.9 %copy-start.10 = (s32[8,8]{1,0:T(8,128)S(1)}, s32[8,8]{1,0:T(8,128)}, u32[]{:S(2)}) copy-start(s32[8,8]{1,0:T(8,128)} %param.12) | copy-start | bytes 772
  0.7 10.7 %copy-start.8 = (s32[2,512]{1,0:T(2,128)S(1)}, s32[2,512]{1,0:T(2,128)}, u32[]{:S(2)}) copy-start(s32[2,512]{1,0:T(2,128)} %param.13) | copy-start | bytes 12292
  2.1 19.9 %copy-start.7 = (bf16[6,3,5,31]{3,1,2,0:T(4,128)(2,1)S(1)}, bf16[6,3,5,31]{3,1,2,0:T(4,128)(2,1)}, u32[]{:S(2)}) copy-start(bf16[6,3,5,31]{3,1,2,0:T(4,128)(2,1)} %param.14) | copy-start | bytes 16744
  3.2 21.2 %collective-permute-start.1 = (bf16[1,256,1024]{2,1,0:T(8,128)(2,1)}, bf16[1,256,1024]{2,1,0:T(8,128)(2,1)S(1)}, u32[]{:S(2)}, u32[]{:S(2)}) collective-permute-start(bf16[1,256,1024]{2,1,0:T(8,128)(2,1)} %get-tuple-element.548), channel_id=1, source_target_pairs={{1,0},{2,1},{3,2},{5,4},{6,5},{7,6},{9,8},{10,9},{11,10},{13,12},{... | collective-permute-start | bytes 1572872 | tf_op jit(solution)/shard_map/ppermute | solution.py:248
  4.5 20.0 %collective-permute-start = (bf16[1,256,1024]{2,1,0:T(8,128)(2,1)}, bf16[1,256,1024]{2,1,0:T(8,128)(2,1)S(1)}, u32[]{:S(2)}, u32[]{:S(2)}) collective-permute-start(bf16[1,256,1024]{2,1,0:T(8,128)(2,1)} %get-tuple-element.549), channel_id=1, source_target_pairs={{0,1},{1,2},{2,3},{4,5},{5,6},{6,7},{8,9},{9,10},{10,11},{12,13},{... | collective-permute-start | bytes 1572872 | tf_op jit(solution)/shard_map/ppermute | solution.py:247
  14.2 10.3 %copy-start.9 = (s32[1,2,256]{2,1,0:T(2,128)S(1)}, s32[1,2,256]{2,1,0:T(2,128)}, u32[]{:S(2)}) copy-start(s32[1,2,256]{2,1,0:T(2,128)} %param.11) | copy-start | bytes 6148
  14.2 10.3 %copy-start.11 = (f32[6]{0:T(128)S(1)}, f32[6]{0:T(128)}, u32[]{:S(2)}) copy-start(f32[6]{0:T(128)} %param.15) | copy-start | bytes 76
  14.3 10.3 %copy-start.12 = (f32[6]{0:T(128)S(1)}, f32[6]{0:T(128)}, u32[]{:S(2)}) copy-start(f32[6]{0:T(128)} %param.17) | copy-start | bytes 76
  24.5 0.8 copy-start.3
  24.6 2.1 %copy-start.5 = (bf16[1,256,1024]{2,1,0:T(8,128)(2,1)}, bf16[1,256,1024]{2,1,0:T(8,128)(2,1)S(1)}, u32[]{:S(2)}) copy-start(bf16[1,256,1024]{2,1,0:T(8,128)(2,1)S(1)} %get-tuple-element.350.top_ref) | copy-start | bytes 1572868 | tf_op jit(solution)/shard_map/cond
  25.5 3.9 %copy-start.1 = (bf16[6,32,2,15,32]{4,3,0,2,1:T(8,128)(2,1)S(1)}, bf16[6,32,2,15,32]{4,3,0,2,1:T(8,128)(2,1)}, u32[]{:S(2)}) copy-start(bf16[6,32,2,15,32]{4,3,0,2,1:T(8,128)(2,1)} %get-tuple-element.504) | copy-start | bytes 1105924 | tf_op jit(solution)/shard_map/cond

commit v3 on v2

--- a/solution.py
+++ b/solution.py
@@ -1,8 +1,8 @@
 import functools
-import math
 
 import jax
 import jax.numpy as jnp
+import numpy as np
 from jax import lax
 from jax.experimental import pallas as pl
 from jax.experimental.pallas import tpu as pltpu
@@ -12,18 +12,18 @@
 F32 = jnp.float32
 STEP_ONE = 32
 STEP_TWO = 16
-CHUNKS = 4
+CHUNKS = 8
 VMEM = 58 * 1024 * 1024
 
 
 def band_matrix(kernels, step, chunks):
     bank, taps = kernels.shape[0], kernels.shape[-1]
     flat = kernels.reshape(bank, -1, taps)
-    out_pos = jnp.arange(step, dtype=jnp.int32)[:, None, None]
-    in_pos = jnp.arange(step * chunks, dtype=jnp.int32)[None, :, None]
-    tap = jnp.arange(taps, dtype=jnp.int32)[None, None, :]
+    out_pos = np.arange(step)[:, None, None]
+    in_pos = np.arange(step * chunks)[None, :, None]
+    tap = np.arange(taps)[None, None, :]
     lead = 16 - taps // 2
-    onehot = (in_pos - out_pos - lead == tap).astype(BF).reshape(step, chunks, step, taps)
+    onehot = jnp.asarray((in_pos - out_pos - lead == tap).reshape(step, chunks, step, taps), BF)
     band = jnp.einsum("kot,ujrt->kujor", flat, onehot, preferred_element_type=F32)
     return band.astype(BF).reshape(bank * step, -1)
 
@@ -148,9 +148,10 @@
     ids = lax.broadcasted_iota(jnp.int32, (rows, width), 0)
     for b in [2] if aligned else range(5):
         place[0 if aligned else b] = jnp.where(ids == spot_ref[b : b + 1, :], 1.0, 0.0).astype(BF)
-    out_id = lax.broadcasted_iota(jnp.int32, (width, width), 0)
+    out_id = lax.broadcasted_iota(jnp.int32, (width, 1), 0)
+    origin = (out_id % folds) * fold_lanes + out_id // folds
     lane = lax.broadcasted_iota(jnp.int32, (width, width), 1)
-    perm[...] = jnp.where((out_id % folds) * fold_lanes + out_id // folds == lane, 1.0, 0.0).astype(BF)
+    perm[...] = jnp.where(origin == lane, 1.0, 0.0).astype(BF)
     per_two = 128 // step_two
 
     def assemble(i, tile):
@@ -186,9 +187,9 @@
         return carry
 
     def restore(m, carry):
-        at = pl.ds(pl.multiple_of(m * 128, 128), 128)
+        at = pl.ds(pl.multiple_of(m * span, span), span)
         turned = nt_dot(perm[...], done[at, :])
-        out_ref[:, :, at] = turned.reshape(fold_lanes, folds, 128).astype(BF)
+        out_ref[:, :, at] = turned.reshape(fold_lanes, folds, span).astype(BF)
         return carry
 
     def chunk_two(i, carry):
@@ -200,7 +201,7 @@
             assemble(i, tile)
         count = span // step_two
         lax.fori_loop(i * count - later, (i + 1) * count - 1 + last, block_two, 0)
-        lax.fori_loop(i * tiles - later, (i + 1) * tiles - 1 + last, restore, 0)
+        lax.fori_loop(i - later, i + last, restore, 0)
         return carry
 
     lax.fori_loop(0, chunks, chunk_two, 0)
@@ -211,12 +212,6 @@
         return carry
 
     lax.fori_loop(0, chunks, finish, 0)
-
-
-def packed_rows(lines, slots, channels, stations):
-    share = channels / stations
-    room = 5.5 * math.sqrt(lines * slots * share * (1 - share))
-    return min(lines * slots, -(-int(lines * slots * share + room) // 16) * 16)
 
 
 def vmem():
@@ -240,7 +235,6 @@
     ends = lax.axis_size("line") - 1
     fold_lanes = lines * slots
     width = shots * fold_lanes
-    capacity = packed_rows(lines, slots, channels, stations)
 
     mask = live_mask[0]
     live = data[0] * mask[..., None].astype(BF)
@@ -255,18 +249,14 @@
     owner = (own_slots // slots).reshape(-1)
     line_ids = jnp.arange(lines, dtype=jnp.int32)[:, None]
     place = (line_ids * slots + own_slots % slots).reshape(-1)
-    ahead = (owner[:, None] == owner[None, :]) & (place[None, :] < place[:, None])
-    rank = jnp.sum(ahead.astype(jnp.int32), axis=1)
     slot_ids = me * slots + jnp.arange(slots, dtype=jnp.int32)
     hits = receiver_slot[:, None, :] == slot_ids[None, :, None]
     station = jnp.sum(jnp.where(hits, jnp.arange(stations, dtype=jnp.int32), 0), axis=-1)
     channel = station[None] - starts[:, :, None]
     covered = (channel >= 0) & (channel < channels)
     covered = covered.reshape(shots, fold_lanes)
-    lower = jnp.tril(jnp.ones((shots, shots), jnp.int32), -1)
+    lower = jnp.asarray(np.tril(np.ones((shots, shots), np.int32), -1))
     fold = jnp.sum(lower[:, :, None] * covered[None].astype(jnp.int32), axis=1)
-    before = jnp.tril(jnp.ones((fold_lanes, fold_lanes), jnp.int32), -1)
-    order = jnp.sum(before[None] * covered[:, None, :].astype(jnp.int32), axis=2)
     fold_ids = jnp.arange(shots, dtype=jnp.int32)[:, None, None]
     takes = covered[None] & (fold[None] == fold_ids)
     shot_ids = jnp.arange(shots, dtype=jnp.int32)[:, None]
@@ -277,12 +267,17 @@
     copies = 1 if fold_lanes % 128 == 0 else 5
     weights = mask.astype(F32)
 
-    def run(size, ident):
-        rows = jnp.where(rank < size, owner * size + rank, -1).reshape(1, lines * channels)
-        source = shot_ids * size + order
+    def places(size):
+        rows = (owner * size + place).reshape(1, lines * channels)
+        source = shot_ids * size + jnp.arange(fold_lanes, dtype=jnp.int32)[None]
         spot = (jnp.sum(jnp.where(takes, source[None] + 1, 0), axis=1) - 1).reshape(width)
         padded = jnp.pad(spot, (2 * fold_lanes, 2 * fold_lanes), constant_values=-1)
         spots = jnp.stack([padded[b * fold_lanes : b * fold_lanes + width] for b in range(5)])
+        return rows, spots
+
+    rows, spots = places(fold_lanes)
+
+    def run(size, ident, rows, spots):
         total = owners * size
         return pl.pallas_call(
             functools.partial(bank_kernel, shots),
@@ -308,15 +303,7 @@
             name="banks",
         )(live, top, bottom, weights, rows, spots, band_one, shot_tau, band_two, receiver_tau)
 
-    if capacity == fold_lanes:
-        out = run(fold_lanes, 0)
-    else:
-        all_channels = jnp.arange(stations, dtype=jnp.int32)[None, None, :] - starts[:, :, None]
-        lit = (all_channels >= 0) & (all_channels < channels)
-        of_owner = receiver_slot[None] // slots == jnp.arange(owners, dtype=jnp.int32)[:, None, None]
-        most = jnp.max(jnp.sum((lit[:, None] & of_owner[None]).astype(jnp.int32), axis=(2, 3)))
-        most = lax.pmax(most, "line")
-        out = lax.cond(most > capacity, lambda: run(fold_lanes, 0), lambda: run(capacity, 1))
+    out = run(fold_lanes, 0, rows, spots)
     return out.reshape(lines, slots, shots, samples)
 
 

time: 93.9 us -> 89.1 us (0.949)
  the two profiles are of different devices: /device:TPU:26 before, /device:TPU:15 now
where the time goes in v3:
time: 89.1 us; the launch traced here: 88.7 us
  Pallas kernels  63.4 us (71%)
  local copies, waits for them, and re-layouts  10.7 us (12%)
  starting transfers between devices  5.3 us (6%)
  between operations  3.96 us (4%)
  other arithmetic  3.79 us (4%)
  matrix products  1.6 us (2%)
    pallas_call x1, Pallas kernels, run(): pl.pallas_call(functools.partial(bank_kernel, shots), out_shape=jax.Shape...  63.4 us
    ppermute x1, starting transfers between devices, per_device(): bottom = lax.ppermute(live[:1], 'line', [(i + 1, i) for i in range(ends)])  4.02 us
    unnamed x23, local copies, waits for them, and re-layouts  4 us
    reshape x3, local copies, waits for them, and re-layouts, band_matrix(): return band.astype(BF).reshape(bank * step, -1)  3.49 us
  transfers between devices with their start and end apart: 2, of which 0 were waited for; matrix products, arithmetic and copies ran while one was open for 9% of the time, Pallas kernels for 0%

profile of v3, /device:TPU:15, one launch (start us, length us, event | category | flops | bytes accessed | tf_op | source)
XLA Modules:
  0.0 88.7 jit_solution(11910421153955632748)
XLA Ops:
  0.0 0.0 copy-start
  0.0 1.4 %convert_bitcast_fusion = (f32[2,256]{1,0:T(2,128)}, bf16[2,256]{1,0:T(2,128)(2,1)S(1)}) fusion(s32[1,2,256]{2,1,0:T(2,128)} %param.12), kind=kLoop, calls=%fused_computation.27 | loop fusion | flops 1024 | bytes 5120 | tf_op jit(solution)/shard_map/convert_element_type | solution.py:268
  1.4 0.0 copy-start.7
  1.4 0.0 copy-start.6
  1.4 0.0 copy-start.5
  1.4 0.0 copy-start.3
  1.4 1.4 %bitcast_multiply_fusion.live_ref = bf16[2,256,1024]{2,1,0:T(8,128)(2,1)S(1)} fusion(bf16[1,2,256,1024]{3,2,1,0:T(8,128)(2,1)} %param.11, bf16[2,256]{1,0:T(2,128)(2,1)S(1)} %get-tuple-element.18), kind=kLoop, calls=%fused_computation.4 | loop fusion | flops 524288 | bytes 2098176 | tf_op jit(solution)/shard_map/mul | solution.py:240
  2.8 0.0 copy-start.1
  2.8 1.2 %fusion.9 = (bf16[1,256,1024]{2,1,0:T(8,128)(2,1)}, bf16[1,256,1024]{2,1,0:T(8,128)(2,1)}) fusion(bf16[2,256,1024]{2,1,0:T(8,128)(2,1)S(1)} %bitcast_multiply_fusion.live_ref), kind=kLoop, calls=%fused_computation.38 | loop fusion | bytes 2097152 | tf_op jit(solution)/shard_map/slice | solution.py:242
  4.0 1.3 %collective-permute-start = (bf16[1,256,1024]{2,1,0:T(8,128)(2,1)}, bf16[1,256,1024]{2,1,0:T(8,128)(2,1)S(1)}, u32[]{:S(2)}, u32[]{:S(2)}) collective-permute-start(bf16[1,256,1024]{2,1,0:T(8,128)(2,1)} %get-tuple-element.8), channel_id=1, source_target_pairs={{0,1},{1,2},{2,3},{4,5},{5,6},{6,7},{8,9},{9,10},{10,11},{12,13},{... | collective-permute-start | bytes 1572872 | tf_op jit(solution)/shard_map/ppermute | solution.py:241
  5.2 4.0 %collective-permute-start.1 = (bf16[1,256,1024]{2,1,0:T(8,128)(2,1)}, bf16[1,256,1024]{2,1,0:T(8,128)(2,1)}, u32[]{:S(2)}, u32[]{:S(2)}) collective-permute-start(bf16[1,256,1024]{2,1,0:T(8,128)(2,1)} %get-tuple-element.7), channel_id=1, source_target_pairs={{1,0},{2,1},{3,2},{5,4},{6,5},{7,6},{9,8},{10,9},{11,10},{13,12},{... | collective-permute-start | bytes 1572872 | tf_op jit(solution)/shard_map/ppermute | solution.py:242
  9.3 0.0 copy-done.7
  9.3 0.1 constant_dynamic-slice_fusion
  9.4 0.1 dynamic_slice.12
  9.4 0.6 fusion.10
  12.6 0.1 sub.42
  12.6 0.1 sub.43
  12.7 0.0 copy-done.6
  12.7 0.2 select_reduce_fusion
  12.9 0.1 sub.40
  13.0 0.1 add_add_fusion
  14.4 0.1 constant_dynamic-slice_fusion.1
  14.5 0.1 broadcast_bitcast_fusion
  14.5 0.0 copy-done.5
  14.5 0.0 copy-done.3
  14.6 0.9 %fusion = bf16[6,32,2,15,32]{4,3,0,2,1:T(8,128)(2,1)S(1)} fusion(bf16[32,2,32,31,1]{3,2,4,1,0:T(8,128)(2,1)S(1)} %copy-done.3, bf16[6,15,31,1,1]{2,0,1,4,3:T(8,128)(2,1)S(1)} %bitcast.45), kind=kOutput, calls=%fused_computation.1 | convolution fusion | flops 11612160 | bytes 501196 | tf_op jit(solution)/shard_map/kot,ujrt->kujor/dot_general | solution.py:27
  15.5 0.0 copy-done.1
  15.5 0.0 copy-start.4
  15.5 0.3 copy.21
  15.8 0.0 copy-start.8
  15.9 2.5 %reshape.249.band_one = bf16[192,960]{1,0:T(8,128)(2,1)} reshape(bf16[6,32,2,15,32]{4,3,2,1,0:T(8,128)(2,1)S(1)} %copy.21) | data formatting | bytes 737280 | tf_op jit(solution)/shard_map/reshape | solution.py:28
  18.3 0.0 copy-done
  18.3 0.0 copy-done.4
  18.3 0.7 fusion.1
  19.0 0.1 copy.30
  19.1 0.9 %reshape.256.band_two = bf16[96,240]{1,0:T(8,128)(2,1)} reshape(bf16[6,16,3,5,16]{4,3,2,1,0:T(8,128)(2,1)S(1)} %copy.30) | data formatting | bytes 92160 | tf_op jit(solution)/shard_map/reshape | solution.py:28
  20.0 0.0 copy-done.8
  20.0 0.1 multiply_reduce_fusion
  20.2 0.6 stack.20.spot_ref
  20.8 0.6 fusion.6.row_ref
  21.4 0.0 collective-permute-done.top_ref
  21.4 0.0 copy-start.2
  21.4 0.0 collective-permute-done.1.bottom_ref
  21.4 0.8 copy-done.2
  22.2 63.4 %banks.1 = bf16[128,8,1024]{2,1,0:T(8,128)(2,1)} custom-call(bf16[2,256,1024]{2,1,0:T(8,128)(2,1)} %copy-done.1, bf16[1,256,1024]{2,1,0:T(8,128)(2,1)} %copy-done.2, bf16[1,256,1024]{2,1,0:T(8,128)(2,1)} %collective-permute-done.1.bottom_ref, f32[2,256]{1,0:T(2,128)} %get-tuple-element.17.mask_ref, s32[1,512]{1,0:T(1,128)} %fusion.6.row_ref, ...), custom_call_target="tpu_custom_call" | custom-call | tf_op jit(solution)/shard_map/banks/pallas_call | solution.py:282
  85.6 3.1 %copy.37 = bf16[2,64,8,1024]{3,2,1,0:T(8,128)(2,1)} copy(bf16[2,64,8,1024]{3,2,1,0:T(8,128)(2,1)} %bitcast.44) | data formatting | bytes 4194304
  (11 shorter events, 0.1 us)
Async XLA Ops:
  0.0 18.3 %copy-start = (bf16[6,5,31]{2,0,1:T(8,128)(2,1)S(1)}, bf16[6,5,31]{2,0,1:T(8,128)(2,1)}, u32[]{:S(2)}) copy-start(bf16[6,5,31]{2,0,1:T(8,128)(2,1)} %param.17) | copy-start | bytes 5584
  1.4 7.9 %copy-start.7 = (s32[8,8]{1,0:T(8,128)S(1)}, s32[8,8]{1,0:T(8,128)}, u32[]{:S(2)}) copy-start(s32[8,8]{1,0:T(8,128)} %param.13) | copy-start | bytes 772
  1.4 11.4 %copy-start.6 = (s32[2,512]{1,0:T(2,128)S(1)}, s32[2,512]{1,0:T(2,128)}, u32[]{:S(2)}) copy-start(s32[2,512]{1,0:T(2,128)} %param.14) | copy-start | bytes 12292
  1.4 13.2 %copy-start.5 = (bf16[6,3,5,31]{3,1,2,0:T(4,128)(2,1)S(1)}, bf16[6,3,5,31]{3,1,2,0:T(4,128)(2,1)}, u32[]{:S(2)}) copy-start(bf16[6,3,5,31]{3,1,2,0:T(4,128)(2,1)} %param.15) | copy-start | bytes 16744
  1.4 13.2 %copy-start.3 = (bf16[32,2,32,31,1]{3,2,4,1,0:T(8,128)(2,1)S(1)}, bf16[32,2,32,31,1]{3,2,4,1,0:T(8,128)(2,1)}, u32[]{:S(2)}) copy-start(bf16[32,2,32,31,1]{3,2,4,1,0:T(8,128)(2,1)} %constant.81) | copy-start | bytes 380932
  2.8 12.7 %copy-start.1 = (bf16[2,256,1024]{2,1,0:T(8,128)(2,1)}, bf16[2,256,1024]{2,1,0:T(8,128)(2,1)S(1)}, u32[]{:S(2)}) copy-start(bf16[2,256,1024]{2,1,0:T(8,128)(2,1)S(1)} %bitcast_multiply_fusion.live_ref) | copy-start | bytes 3145732
  4.0 17.5 %collective-permute-start = (bf16[1,256,1024]{2,1,0:T(8,128)(2,1)}, bf16[1,256,1024]{2,1,0:T(8,128)(2,1)S(1)}, u32[]{:S(2)}, u32[]{:S(2)}) collective-permute-start(bf16[1,256,1024]{2,1,0:T(8,128)(2,1)} %get-tuple-element.8), channel_id=1, source_target_pairs={{0,1},{1,2},{2,3},{4,5},{5,6},{6,7},{8,9},{9,10},{10,11},{12,13},{... | collective-permute-start | bytes 1572872 | tf_op jit(solution)/shard_map/ppermute | solution.py:241
  5.2 16.2 %collective-permute-start.1 = (bf16[1,256,1024]{2,1,0:T(8,128)(2,1)}, bf16[1,256,1024]{2,1,0:T(8,128)(2,1)}, u32[]{:S(2)}, u32[]{:S(2)}) collective-permute-start(bf16[1,256,1024]{2,1,0:T(8,128)(2,1)} %get-tuple-element.7), channel_id=1, source_target_pairs={{1,0},{2,1},{3,2},{5,4},{6,5},{7,6},{9,8},{10,9},{11,10},{13,12},{... | collective-permute-start | bytes 1572872 | tf_op jit(solution)/shard_map/ppermute | solution.py:242
  15.5 2.8 %copy-start.4 = (bf16[16,3,16,31,1]{3,2,4,1,0:T(8,128)(2,1)S(1)}, bf16[16,3,16,31,1]{3,2,4,1,0:T(8,128)(2,1)}, u32[]{:S(2)}) copy-start(bf16[16,3,16,31,1]{3,2,4,1,0:T(8,128)(2,1)} %constant.82) | copy-start | bytes 142852
  15.8 4.2 %copy-start.8 = (s32[8,8]{1,0:T(8,128)S(1)}, s32[8,8]{1,0:T(8,128)}, u32[]{:S(2)}) copy-start(s32[8,8]{1,0:T(8,128)} %constant.73.clone) | copy-start | bytes 772
  21.4 0.8 copy-start.2
